TPU v7x, 512 devices: a whole 4x4x16 slice. The times are simulated.
512 devices in a mesh: dp: 64 (over x, z), mp: 8 (over y, core).
Axes of the slice: x: 4, y: 4, z: 16, core: 2. Of those that a mesh axis runs over, the one named last changes fastest.
Arguments:
- latent_in: bfloat16 [64, 34, 32, 1280], P('dp', None, None, 'mp'), may hold values from -6 to 6
- out_grad: bfloat16 [64, 32, 32, 1280], P('dp'), may hold values from -2.5 to 2.5
- q_prev: bfloat16 [9, 1280, 64], P(None, 'mp'), may hold values from -6 to 6
Outputs:
- p_factor: float32 [1280, 64], P('dp')
- q_factor: float32 [9, 1280, 64], P(None, 'mp')
All inputs are finite; a program needn't handle non-finite values.
Results may differ from a plain program's by a relative error of at most 0.0003.
Values sent between devices are 32-bit elements; how exact they have to be, the bound alone decides.
No kernel may reach another device: no remote copies, remote signals or barrier semaphores. Data moves between devices by JAX's collectives and lax.ppermute only.
A program may use at most 64 MiB of HBM per device.

v0:
```python
import math

import jax
import jax.numpy as jnp
from jax import lax
from jax.sharding import PartitionSpec as P


def body(latent_in, out_grad, q_prev):
    row_count = out_grad.shape[1]
    col_count = out_grad.shape[2]
    out_width = out_grad.shape[3]
    tap_count, cin_local, rank_width = q_prev.shape
    padded = jnp.pad(latent_in[0], ((0, 0), (1, 1), (0, 0)))
    pieces = [
        padded[tap_row : tap_row + row_count, tap_col : tap_col + col_count, :].reshape(
            row_count * col_count, cin_local
        )
        for tap_row in range(3)
        for tap_col in range(3)
    ]
    columns = jnp.concatenate(pieces, axis=1)
    grads = out_grad[0].reshape(row_count * col_count, out_width)
    weight_grad = lax.dot_general(
        columns, grads, (((0,), (0,)), ((), ())), preferred_element_type=jnp.float32
    )
    q_basis = q_prev.reshape(tap_count * cin_local, rank_width).astype(jnp.float32)
    partial_p = lax.dot_general(
        weight_grad,
        q_basis,
        (((0,), (0,)), ((), ())),
        precision=lax.Precision.HIGHEST,
        preferred_element_type=jnp.float32,
    )
    unit_scale = math.sqrt(out_width)
    row_block = lax.psum_scatter(partial_p, "dp", scatter_dimension=0, tiled=True)
    row_block = lax.psum(row_block, "mp")
    gram_matrix = lax.psum(jnp.dot(row_block.T, row_block, precision=lax.Precision.HIGHEST), "dp")
    factor_low = jnp.linalg.cholesky(gram_matrix)
    own_rows = (
        unit_scale
        * lax.linalg.triangular_solve(factor_low, row_block.T, left_side=True, lower=True).T
    )
    full_p = lax.all_gather(own_rows, "dp", axis=0, tiled=True)
    q_part = jnp.dot(weight_grad, full_p, precision=lax.Precision.HIGHEST) / out_width
    q_factor = lax.psum(q_part, "dp").reshape(tap_count, cin_local, rank_width)
    return (own_rows, q_factor)


def solution(mesh):
    placed = (P("dp", None, None, "mp"), P("dp", None, None, None), P(None, "mp", None))
    return jax.shard_map(
        body,
        mesh=mesh,
        in_specs=placed,
        out_specs=(P("dp", None), P(None, "mp", None)),
        check_vma=False,
    )
```

profile of v0, /device:TPU:8, one launch (start us, length us, event | category | flops | bytes accessed | tf_op | source)
XLA Modules:
  0.0 1001.0 jit_solution(4820168020929551438)
XLA Ops:
  7.2 0.0 copy-start
  7.2 0.0 all-reduce.7.cloned.1.call-start
  7.2 2.8 fusion.3
  10.0 5.2 pad_slice_fusion
  15.2 1.2 copy.13
  16.4 7.1 concatenate.3
  23.5 0.0 copy-done
  23.5 6.1 fusion.4
  29.6 3.0 copy-done.1
  32.6 7.4 fusion.5
  40.0 0.0 all-reduce.7.cloned.1.call-update
  40.0 0.0 all-reduce.5.cloned.1.call-start
  40.1 1.3 dynamic-slice
  42.0 268.5 %all-reduce.7.cloned.1.call-done = f32[1280,64]{1,0:T(8,128)} async-done(((f32[1280,64]{1,0:T(8,128)}), f32[1280,64]{1,0:T(8,128)}) %all-reduce.7.cloned.1.call-update) | async-done | bytes 327696
  310.5 0.7 constant_dynamic-slice_fusion
  311.2 20.8 %psum.21 = f32[20,64]{1,0:T(8,128)S(1)} all-reduce(f32[20,64]{1,0:T(8,128)S(1)} %constant_dynamic-slice_fusion), channel_id=1, replica_groups=mesh['dp'=64,'mp'=8] {'mp'}, use_global_device_ids=true, to_apply=%region_1.2 | all-reduce | flops 1280 | bytes 10240 | tf_op jit(solution)/shard_map/psum | solution.py:37
  332.0 0.2 fusion.6
  332.3 276.7 %psum.22 = f32[64,64]{0,1:T(8,128)S(1)} all-reduce(f32[64,64]{0,1:T(8,128)S(1)} %fusion.6), channel_id=1, replica_groups=mesh['dp'=64,'mp'=8] {'dp'}, use_global_device_ids=true, to_apply=%region_2.3 | all-reduce | flops 4096 | bytes 32768 | tf_op jit(solution)/shard_map/psum | solution.py:38
  608.9 0.1 copy.15
  609.0 5.8 cholesky.16
  614.9 0.6 compare_reduce_fusion
  615.5 0.7 fusion
  616.2 4.9 custom-call.6
  621.1 0.2 convolution_multiply_fusion.1
  621.3 0.0 copy-start.2
  621.3 96.9 %all-gather = f32[64,20,64]{2,1,0:T(8,128)S(1)} all-gather(f32[1,20,64]{2,1,0:T(8,128)S(1)} %bitcast.46), channel_id=1, replica_groups=mesh['dp'=64,'mp'=8] {'dp'}, dimensions={0}, use_global_device_ids=true | all-gather | bytes 332800 | tf_op jit(solution)/shard_map/all_gather | solution.py:44
  718.2 0.9 reshape.64
  719.1 9.2 convolution_multiply_fusion
  728.3 1.1 copy.16
  729.4 0.0 all-reduce.5.cloned.1.call-update
  729.4 262.5 %all-reduce.5.cloned.1.call-done = f32[9,160,64]{2,1,0:T(8,128)} async-done(((f32[9,160,64]{2,1,0:T(8,128)}), f32[9,160,64]{2,1,0:T(8,128)}) %all-reduce.5.cloned.1.call-update) | async-done | bytes 368656 | tf_op jit(solution)/shard_map/psum | solution.py:46
  991.9 2.3 copy.17
  (4 shorter events, 0.0 us)
Async XLA Ops:
  7.2 16.3 %copy-start = (bf16[1,32,32,1280]{3,2,1,0:T(8,128)(2,1)S(1)}, bf16[1,32,32,1280]{3,2,1,0:T(8,128)(2,1)}, u32[]{:S(2)}) copy-start(bf16[1,32,32,1280]{3,2,1,0:T(8,128)(2,1)} %param.4) | copy-start | bytes 7864324
  7.2 303.3 %all-reduce.7.cloned.1.call-start = ((), (), s32[]{:S(2)}) async-start(), calls=%async_computation.1 | async-start | bytes 1310720
  29.6 3.0 copy-start.1
  40.0 951.9 %all-reduce.5.cloned.1.call-start = ((), (), s32[]{:S(2)}) async-start(), calls=%async_computation | async-start | bytes 1474560 | tf_op jit(solution)/shard_map/psum | solution.py:46
  621.3 372.9 %copy-start.2 = (f32[20,64]{1,0:T(8,128)}, f32[20,64]{1,0:T(8,128)S(1)}, u32[]{:S(2)}) copy-start(f32[20,64]{1,0:T(8,128)S(1)} %convolution_multiply_fusion.1) | copy-start | bytes 15364
Sparse Core Ops, SparseCore 0:
  40.1 270.3 all-reduce.6
  729.5 262.2 all-reduce.4
where the time goes:
time: 1000 us
  waiting for transfers between devices  531 us (53%)
  blocking collectives  394 us (39%)
  local copies, waits for them, and re-layouts  25.6 us (3%)
  matrix products  23.1 us (2%)
  between operations  14.8 us (1%)
  other arithmetic  12.1 us (1%)
    psum x1, blocking collectives, body(): lax.psum(jnp.dot(row_block.T, row_block, precision=lax.Precision.HIGHEST)...  277 us
    unnamed x3, waiting for transfers between devices  269 us
    psum x1, waiting for transfers between devices, body(): q_factor = lax.psum(q_part, 'dp').reshape(tap_count, cin_local, rank_width)  262 us
    all_gather x1, blocking collectives, body(): full_p = lax.all_gather(own_rows, 'dp', axis=0, tiled=True)  96.9 us
    psum x1, blocking collectives, body(): row_block = lax.psum(row_block, 'mp')  20.8 us
  transfers between devices with their start and end apart: 2, of which 2 were waited for; matrix products, arithmetic and copies ran while one was open for 0% of the time, Pallas kernels for 0%

commit v1 on v0

v1 whole, which is shorter than its diff:
```python
import math

import jax
import jax.numpy as jnp
from jax import lax
from jax.experimental import pallas as pl
from jax.experimental.pallas import tpu as pltpu
from jax.sharding import Mesh
from jax.sharding import PartitionSpec as P

F32 = jnp.float32
BF16 = jnp.bfloat16
VMEM = pl.BlockSpec(memory_space=pltpu.VMEM)
ANY = pl.BlockSpec(memory_space=pl.ANY)


def parts_of(value):
    high = value.astype(BF16)
    rest = value - high.astype(F32)
    middle = rest.astype(BF16)
    low = (rest - middle.astype(F32)).astype(BF16)
    return high, middle, low


def dot(left, right, dims):
    return lax.dot_general(left, right, (dims, ((), ())), preferred_element_type=F32)


def left_kernel(width, x_ref, g_hbm, q_ref, out_ref, g_ref, sem):
    load = pltpu.make_async_copy(g_hbm, g_ref, sem)
    load.start()
    pixels, rank = g_ref.shape[0], q_ref.shape[2]
    taps = None
    for a in range(3):
        basis = jnp.concatenate([q_ref[3 * a + b] for b in range(3)], axis=1)
        term = dot(x_ref[width * a : width * a + pixels, :], basis, ((1,), (0,)))
        taps = term if taps is None else taps + term
    column = lax.broadcasted_iota(jnp.int32, (pixels, rank), 0) & (width - 1)
    before = pltpu.roll(taps[:, :rank], 1, 0)
    after = pltpu.roll(taps[:, 2 * rank :], pixels - 1, 0)
    projected = (
        taps[:, rank : 2 * rank]
        + jnp.where(column == 0, 0.0, before)
        + jnp.where(column == width - 1, 0.0, after)
    )
    stacked = jnp.concatenate(parts_of(projected.T), axis=0)
    load.wait()
    total = dot(stacked, g_ref[...], ((1,), (0,)))
    total = total[:rank] + total[rank : 2 * rank] + total[2 * rank :]
    rows = out_ref.shape[1]
    for i in range(out_ref.shape[0]):
        out_ref[i] = total[rows * i : rows * (i + 1)]


def gather_rows(pieces_ref, whole_ref):
    rows = pieces_ref.shape[1]
    for i in range(pieces_ref.shape[0]):
        whole_ref[rows * i : rows * (i + 1), :] = pieces_ref[i]


def right_kernel(width, p_ref, x_ref, g_hbm, out_ref, whole_ref, g_ref, sem):
    load = pltpu.make_async_copy(g_hbm, g_ref, sem)
    load.start()
    gather_rows(p_ref, whole_ref)
    rank, pixels = whole_ref.shape[0], g_ref.shape[0]
    cin = x_ref.shape[1]
    stacked = jnp.concatenate(parts_of(whole_ref[...]), axis=0)
    load.wait()
    mapped = dot(stacked, g_ref[...], ((1,), (1,)))
    mapped = mapped[:rank] + mapped[rank : 2 * rank] + mapped[2 * rank :]
    column = lax.broadcasted_iota(jnp.int32, (rank, pixels), 1) & (width - 1)
    ahead = jnp.where(column == width - 1, 0.0, pltpu.roll(mapped, pixels - 1, 1))
    behind = jnp.where(column == 0, 0.0, pltpu.roll(mapped, 1, 1))
    shifted = jnp.concatenate(
        [part for side in (ahead, mapped, behind) for part in parts_of(side)], axis=0
    )
    pieces = []
    for a in range(3):
        term = dot(shifted, x_ref[width * a : width * a + pixels, :], ((1,), (0,)))
        for b in range(3):
            t = term[3 * rank * b : 3 * rank * (b + 1)]
            pieces.append(t[:rank] + t[rank : 2 * rank] + t[2 * rank :])
    whole = jnp.concatenate(pieces, axis=1)
    groups, rows = out_ref.shape[0], out_ref.shape[1]
    for i in range(groups):
        out_ref[i] = whole[rows * i : rows * (i + 1)]


def factor_kernel(scale, p_ref, inverse_ref, factor_ref, whole_ref):
    gather_rows(p_ref, whole_ref)
    whole = whole_ref[...]
    rank = whole.shape[0]
    gram = lax.dot_general(
        whole,
        whole,
        (((1,), (1,)), ((), ())),
        precision=lax.Precision.HIGHEST,
        preferred_element_type=F32,
    )
    row = lax.broadcasted_iota(jnp.int32, (rank, rank), 0)
    col = lax.broadcasted_iota(jnp.int32, (rank, rank), 1)
    eye = row == col
    work = jnp.concatenate([gram, jnp.where(eye, 1.0, 0.0)], axis=1)
    below = lax.broadcasted_iota(jnp.int32, (rank, 1), 0)
    for j in range(rank - 1):
        pivot_row = work[j : j + 1, :]
        pivot_row = pivot_row / work[j : j + 1, j : j + 1]
        multiplier = jnp.where(below > j, work[:, j : j + 1], 0.0)
        work = work - multiplier * pivot_row
    diagonal = jnp.sum(jnp.where(eye, work[:, :rank], 0.0), axis=1, keepdims=True)
    inverse = work[:, rank:] / jnp.sqrt(diagonal)
    inverse_ref[...] = inverse
    rows = lax.dot_general(
        inverse,
        whole,
        (((1,), (0,)), ((), ())),
        precision=lax.Precision.HIGHEST,
        preferred_element_type=F32,
    )
    factor_ref[...] = (scale * rows).T


def finish_kernel(scale, q_ref, inverse_ref, out_ref):
    groups = q_ref.shape[0]
    raw = jnp.concatenate([q_ref[i] for i in range(groups)], axis=0)
    high, middle, low = parts_of(raw)
    inv_high, inv_middle, inv_low = parts_of(inverse_ref[...])
    left = jnp.concatenate([inv_high, inv_middle, inv_high, inv_high], axis=1)
    right = jnp.concatenate([high, high, middle, low], axis=0)
    out_ref[...] = (scale * dot(left, right, ((1,), (0,)))).T


def solution(mesh):
    n_x, n_z, n_y, n_c = 4, 16, 4, 2
    grid = Mesh(mesh.devices.reshape(n_x, n_z, n_y, n_c), ("x", "z", "y", "c"))
    planes = ("x", "y", "c")
    n_plane = n_x * n_y * n_c

    def call(kernel, out_shape, in_specs, scratch, flops, moved):
        return pl.pallas_call(
            kernel,
            out_shape=out_shape,
            in_specs=in_specs,
            out_specs=jax.tree.map(lambda _: VMEM, out_shape),
            scratch_shapes=scratch,
            compiler_params=pltpu.CompilerParams(vmem_limit_bytes=40 * 2**20),
            cost_estimate=pl.CostEstimate(flops=flops, bytes_accessed=moved, transcendentals=0),
        )

    def exchange(blocks, axes):
        return lax.all_to_all(blocks, axes, 0, 0, tiled=True)

    def to_all(block, axes, count):
        return exchange(jnp.broadcast_to(block[None], (count,) + block.shape), axes)

    def body(latent_in, out_grad, q_prev):
        rows, width, cout = out_grad.shape[1:]
        taps, cin, rank = q_prev.shape
        pixels = rows * width
        x = latent_in.reshape(-1, cin)
        g = out_grad.reshape(pixels, cout)
        g_scratch = [pltpu.VMEM((pixels, cout), BF16), pltpu.SemaphoreType.DMA]
        whole_p = pltpu.VMEM((rank, cout), F32)
        own = rank // n_plane

        p_term = call(
            lambda *refs: left_kernel(width, *refs),
            jax.ShapeDtypeStruct((n_plane, own, cout), F32),
            [VMEM, ANY, VMEM],
            g_scratch,
            2 * pixels * cout * 256,
            2 * pixels * cout,
        )(x, g, q_prev)
        piece = jnp.sum(exchange(p_term, planes), axis=0)
        piece = jnp.sum(to_all(piece, "z", n_z), axis=0)
        p_pieces = to_all(piece, planes, n_plane)

        q_term = call(
            lambda *refs: right_kernel(width, *refs),
            jax.ShapeDtypeStruct((n_x, rank // n_x, taps * cin), F32),
            [VMEM, VMEM, ANY],
            [whole_p] + g_scratch,
            4 * pixels * cout * 256,
            2 * pixels * cout,
        )(p_pieces, x, g)

        inverse, p_whole = call(
            lambda *refs: factor_kernel(math.sqrt(cout), *refs),
            (jax.ShapeDtypeStruct((rank, rank), F32), jax.ShapeDtypeStruct((cout, rank), F32)),
            [VMEM],
            [whole_p],
            2 * pixels * cout * 256,
            2 * pixels * cout,
        )(p_pieces)
        share = cout // (n_x * n_z)
        at = (lax.axis_index("x") * n_z + lax.axis_index("z")) * share
        p_factor = lax.dynamic_slice_in_dim(p_whole, at, share, axis=0)

        part = jnp.sum(exchange(q_term, "x"), axis=0)
        part = part.reshape(n_z, rank // (n_x * n_z), taps * cin)
        part = jnp.sum(exchange(part, "z"), axis=0)
        part = to_all(part, "z", n_z).reshape(rank // n_x, taps * cin)
        q_raw = to_all(part, "x", n_x)

        q_factor = call(
            lambda *refs: finish_kernel(1.0 / math.sqrt(cout), *refs),
            jax.ShapeDtypeStruct((taps * cin, rank), F32),
            [VMEM, VMEM],
            [],
            2 * taps * cin * rank * 256,
            8 * taps * cin * rank,
        )(q_raw, inverse)
        return p_factor, q_factor.reshape(taps, cin, rank)

    sample, channel = ("x", "z"), ("y", "c")
    return jax.shard_map(
        body,
        mesh=grid,
        in_specs=(P(sample, None, None, channel), P(sample, None, None, None), P(None, channel, None)),
        out_specs=(P(sample, None), P(None, channel, None)),
        check_vma=False,
    )
```

time: 1000 us -> 130 us (0.13)
  the two profiles are of different devices: /device:TPU:8 before, /device:TPU:2 now
where the time goes in v1:
time: 130 us
  blocking collectives  105 us (81%)
  Pallas kernels  12.3 us (9%)
  local copies, waits for them, and re-layouts  6.83 us (5%)
  starting transfers between devices  4.89 us (4%)
    all_to_all x6, blocking collectives, exchange(): return lax.all_to_all(blocks, axes, 0, 0, tiled=True)  105 us
    pallas_call x1, Pallas kernels, body(): call(lambda *refs: factor_kernel(math.sqrt(cout), *refs), (jax.ShapeDtype...  6.75 us
    unnamed x11, local copies, waits for them, and re-layouts  5.2 us
    all_to_all x1, starting transfers between devices, exchange(): return lax.all_to_all(blocks, axes, 0, 0, tiled=True)  4.89 us
  transfers between devices with their start and end apart: 1, of which 0 were waited for; matrix products, arithmetic and copies ran while one was open for 0% of the time, Pallas kernels for 5%

profile of v1, /device:TPU:2, one launch (start us, length us, event | category | flops | bytes accessed | tf_op | source)
XLA Modules:
  0.0 129.7 jit_solution(8162767416649919666)
XLA Ops:
  0.6 1.2 copy.11.refs_2_
  1.8 0.0 copy-start
  1.9 1.7 %copy-done = bf16[1,32,32,1280]{3,2,1,0:T(8,128)(2,1)S(1)} copy-done((bf16[1,32,32,1280]{3,2,1,0:T(8,128)(2,1)S(1)}, bf16[1,32,32,1280]{3,2,1,0:T(8,128)(2,1)}, u32[]{:S(2)}) %copy-start) | copy-done | bytes 2621464
  3.6 0.0 copy-start.2
  3.6 1.1 copy-done.2
  4.6 0.0 copy-start.1
  4.7 0.0 copy-start.3
  4.7 2.5 %shard_map.50 = f32[32,2,1280]{2,1,0:T(2,128)S(1)} custom-call(bf16[1088,160]{1,0:T(8,128)(2,1)S(1)} %bitcast.9, bf16[1024,1280]{1,0:T(8,128)(2,1)S(1)} %bitcast.7, bf16[9,160,64]{2,1,0:T(8,128)(2,1)S(1)} %copy.11.refs_2_), custom_call_target="tpu_custom_call" | custom-call | flops 671088640 | bytes 2621440 | tf_op jit(solution)/shard_map/pallas_call | solution.py:166
  7.2 16.9 %all_to_all.35 = f32[32,2,1280]{2,1,0:T(2,128)S(1)} all-to-all(f32[32,2,1280]{2,1,0:T(2,128)S(1)} %shard_map.50), channel_id=1, replica_groups=mesh['x'=4,'z'=16,'y'=4,'c'=2] {'x','y','c'}, dimensions={0} | all-to-all | bytes 655360 | tf_op jit(solution)/shard_map/all_to_all | solution.py:151
  24.1 0.1 reduce_sum.36
  24.3 28.5 %all_to_all.36 = f32[16,2,1280]{2,1,0:T(2,128)S(1)} all-to-all(f32[16,2,1280]{2,1,0:T(2,128)S(1)} %broadcast_in_dim.10), channel_id=1, replica_groups=mesh['x'=4,'z'=16,'y'=4,'c'=2] {'z'}, dimensions={0} | all-to-all | bytes 327680 | tf_op jit(solution)/shard_map/all_to_all | solution.py:151
  52.8 0.1 reduce_sum.37
  52.8 0.1 broadcast_in_dim.11
  52.9 13.8 %all_to_all.37.refs_0_ = f32[32,2,1280]{2,1,0:T(2,128)S(1)} all-to-all(f32[32,2,1280]{2,1,0:T(2,128)S(1)} %broadcast_in_dim.11), channel_id=1, replica_groups=mesh['x'=4,'z'=16,'y'=4,'c'=2] {'x','y','c'}, dimensions={0} | all-to-all | bytes 655360 | tf_op jit(solution)/shard_map/all_to_all | solution.py:151
  66.7 0.0 copy-done.1
  66.7 0.0 copy-done.3
  66.7 2.5 %shard_map.52 = f32[4,16,1440]{2,1,0:T(8,128)S(1)} custom-call(f32[32,2,1280]{2,1,0:T(2,128)S(1)} %all_to_all.37.refs_0_, bf16[1088,160]{1,0:T(8,128)(2,1)S(1)} %bitcast.10, bf16[1024,1280]{1,0:T(8,128)(2,1)S(1)} %bitcast.8), custom_call_target="tpu_custom_call" | custom-call | flops 1342177280 | bytes 2621440 | tf_op jit(solution)/shard_map/pallas_call | solution.py:178
  69.2 11.4 %all_to_all.38 = f32[4,16,1440]{2,1,0:T(8,128)S(1)} all-to-all(f32[4,16,1440]{2,1,0:T(8,128)S(1)} %shard_map.52), channel_id=1, replica_groups=mesh['x'=4,'z'=16,'y'=4,'c'=2] {'x'}, dimensions={0} | all-to-all | bytes 737280 | tf_op jit(solution)/shard_map/all_to_all | solution.py:151
  80.6 0.1 reshape.26
  80.7 17.8 %all_to_all.39 = f32[16,1,1440]{2,1,0:T(1,128)S(1)} all-to-all(f32[16,1,1440]{2,1,0:T(1,128)S(1)} %reshape.26), channel_id=1, replica_groups=mesh['x'=4,'z'=16,'y'=4,'c'=2] {'z'}, dimensions={0} | all-to-all | bytes 184320 | tf_op jit(solution)/shard_map/all_to_all | solution.py:151
  98.5 0.1 reduce_sum.39
  98.6 0.1 broadcast_in_dim.12
  98.6 16.4 %all_to_all.40 = f32[16,1,1440]{2,1,0:T(1,128)S(1)} all-to-all(f32[16,1,1440]{2,1,0:T(1,128)S(1)} %broadcast_in_dim.12), channel_id=1, replica_groups=mesh['x'=4,'z'=16,'y'=4,'c'=2] {'z'}, dimensions={0} | all-to-all | bytes 184320 | tf_op jit(solution)/shard_map/all_to_all | solution.py:151
  115.0 0.8 broadcast_in_dim.14
  115.8 4.9 %all-to-all-start.6 = ((f32[4,16,1440]{2,1,0:T(8,128)}), f32[4,16,1440]{2,1,0:T(8,128)S(1)}, u32[]{:S(2)}, u32[]{:S(2)}) async-start(f32[4,16,1440]{2,1,0:T(8,128)} %broadcast_in_dim.14), calls=%async_computation.6 | async-start | bytes 786432 | tf_op jit(solution)/shard_map/all_to_all | solution.py:151
  120.7 6.7 %shard_map.51 = (f32[64,64]{1,0:T(8,128)S(1)}, f32[1280,64]{1,0:T(8,128)S(1)}) custom-call(f32[32,2,1280]{2,1,0:T(2,128)S(1)} %all_to_all.37.refs_0_), custom_call_target="tpu_custom_call" | custom-call | flops 671088640 | bytes 2621440 | tf_op jit(solution)/shard_map/pallas_call | solution.py:187
  127.4 0.6 constant_dynamic-slice_fusion
  128.0 0.0 all-to-all-done.6.refs_0_
  128.0 0.5 shard_map.53
  128.5 1.2 copy.13
  (3 shorter events, 0.1 us)
Async XLA Ops:
  1.8 1.7 %copy-start = (bf16[1,32,32,1280]{3,2,1,0:T(8,128)(2,1)S(1)}, bf16[1,32,32,1280]{3,2,1,0:T(8,128)(2,1)}, u32[]{:S(2)}) copy-start(bf16[1,32,32,1280]{3,2,1,0:T(8,128)(2,1)} %param.4) | copy-start | bytes 7864324
  3.6 1.1 copy-start.2
  4.6 62.1 %copy-start.1 = (bf16[1,32,32,1280]{3,2,1,0:T(8,128)(2,1)S(1)}, bf16[1,32,32,1280]{3,2,1,0:T(8,128)(2,1)}, u32[]{:S(2)}) copy-start(bf16[1,32,32,1280]{3,2,1,0:T(8,128)(2,1)} %param.4) | copy-start | bytes 7864324
  4.7 62.1 %copy-start.3 = (bf16[1,34,32,160]{3,2,1,0:T(8,128)(2,1)S(1)}, bf16[1,34,32,160]{3,2,1,0:T(8,128)(2,1)}, u32[]{:S(2)}) copy-start(bf16[1,34,32,160]{3,2,1,0:T(8,128)(2,1)} %param.3) | copy-start | bytes 1044484
  115.8 12.3 %all-to-all-start.6 = ((f32[4,16,1440]{2,1,0:T(8,128)}), f32[4,16,1440]{2,1,0:T(8,128)S(1)}, u32[]{:S(2)}, u32[]{:S(2)}) async-start(f32[4,16,1440]{2,1,0:T(8,128)} %broadcast_in_dim.14), calls=%async_computation.6 | async-start | bytes 786432 | tf_op jit(solution)/shard_map/all_to_all | solution.py:151

commit v2 on v1

--- a/solution.py
+++ b/solution.py
@@ -11,7 +11,7 @@
 F32 = jnp.float32
 BF16 = jnp.bfloat16
 VMEM = pl.BlockSpec(memory_space=pltpu.VMEM)
-ANY = pl.BlockSpec(memory_space=pl.ANY)
+HBM = pl.BlockSpec(memory_space=pltpu.HBM)
 
 
 def parts_of(value):
@@ -26,25 +26,31 @@
     return lax.dot_general(left, right, (dims, ((), ())), preferred_element_type=F32)
 
 
-def left_kernel(width, x_ref, g_hbm, q_ref, out_ref, g_ref, sem):
-    load = pltpu.make_async_copy(g_hbm, g_ref, sem)
-    load.start()
-    pixels, rank = g_ref.shape[0], q_ref.shape[2]
+def left_kernel(width, x_hbm, q_hbm, g_hbm, out_ref, x_ref, q_ref, g_ref, sems):
+    loads = [
+        pltpu.make_async_copy(source, target, sems.at[i])
+        for i, (source, target) in enumerate(((x_hbm, x_ref), (q_hbm, q_ref), (g_hbm, g_ref)))
+    ]
+    for load in loads:
+        load.start()
+    loads[0].wait()
+    loads[1].wait()
+    pixels, rank, cin = g_ref.shape[0], q_ref.shape[1], q_ref.shape[2]
     taps = None
     for a in range(3):
-        basis = jnp.concatenate([q_ref[3 * a + b] for b in range(3)], axis=1)
-        term = dot(x_ref[width * a : width * a + pixels, :], basis, ((1,), (0,)))
+        basis = q_ref[3 * a : 3 * a + 3].reshape(3 * rank, cin)
+        term = dot(basis, x_ref[width * a : width * a + pixels, :], ((1,), (1,)))
         taps = term if taps is None else taps + term
-    column = lax.broadcasted_iota(jnp.int32, (pixels, rank), 0) & (width - 1)
-    before = pltpu.roll(taps[:, :rank], 1, 0)
-    after = pltpu.roll(taps[:, 2 * rank :], pixels - 1, 0)
+    column = lax.broadcasted_iota(jnp.int32, (rank, pixels), 1) & (width - 1)
+    before = pltpu.roll(taps[:rank], 1, 1)
+    after = pltpu.roll(taps[2 * rank :], pixels - 1, 1)
     projected = (
-        taps[:, rank : 2 * rank]
+        taps[rank : 2 * rank]
         + jnp.where(column == 0, 0.0, before)
         + jnp.where(column == width - 1, 0.0, after)
     )
-    stacked = jnp.concatenate(parts_of(projected.T), axis=0)
-    load.wait()
+    stacked = jnp.concatenate(parts_of(projected), axis=0)
+    loads[2].wait()
     total = dot(stacked, g_ref[...], ((1,), (0,)))
     total = total[:rank] + total[rank : 2 * rank] + total[2 * rank :]
     rows = out_ref.shape[1]
@@ -58,14 +64,10 @@
         whole_ref[rows * i : rows * (i + 1), :] = pieces_ref[i]
 
 
-def right_kernel(width, p_ref, x_ref, g_hbm, out_ref, whole_ref, g_ref, sem):
-    load = pltpu.make_async_copy(g_hbm, g_ref, sem)
-    load.start()
+def right_kernel(width, p_ref, x_ref, g_ref, out_ref, whole_ref):
     gather_rows(p_ref, whole_ref)
     rank, pixels = whole_ref.shape[0], g_ref.shape[0]
-    cin = x_ref.shape[1]
     stacked = jnp.concatenate(parts_of(whole_ref[...]), axis=0)
-    load.wait()
     mapped = dot(stacked, g_ref[...], ((1,), (1,)))
     mapped = mapped[:rank] + mapped[rank : 2 * rank] + mapped[2 * rank :]
     column = lax.broadcasted_iota(jnp.int32, (rank, pixels), 1) & (width - 1)
@@ -127,31 +129,38 @@
     inv_high, inv_middle, inv_low = parts_of(inverse_ref[...])
     left = jnp.concatenate([inv_high, inv_middle, inv_high, inv_high], axis=1)
     right = jnp.concatenate([high, high, middle, low], axis=0)
-    out_ref[...] = (scale * dot(left, right, ((1,), (0,)))).T
+    whole = scale * dot(left, right, ((1,), (0,)))
+    cin = out_ref.shape[2]
+    for k in range(out_ref.shape[0]):
+        out_ref[k] = whole[:, cin * k : cin * (k + 1)]
 
 
 def solution(mesh):
-    n_x, n_z, n_y, n_c = 4, 16, 4, 2
-    grid = Mesh(mesh.devices.reshape(n_x, n_z, n_y, n_c), ("x", "z", "y", "c"))
-    planes = ("x", "y", "c")
-    n_plane = n_x * n_y * n_c
-
-    def call(kernel, out_shape, in_specs, scratch, flops, moved):
+    sizes = {"x": 4, "far": 8, "near": 2, "y": 4, "c": 2}
+    grid = Mesh(mesh.devices.reshape(tuple(sizes.values())), tuple(sizes))
+
+    def count(axes):
+        return math.prod(sizes[axis] for axis in axes)
+
+    sample, channel = ("x", "far", "near"), ("y", "c")
+    p_split, q_split, rest = ("x", "near", "y", "c"), ("x", "near"), ("far",)
+
+    def call(kernel, out_shape, in_specs, scratch, flops, moved, grant=40):
         return pl.pallas_call(
             kernel,
             out_shape=out_shape,
             in_specs=in_specs,
             out_specs=jax.tree.map(lambda _: VMEM, out_shape),
             scratch_shapes=scratch,
-            compiler_params=pltpu.CompilerParams(vmem_limit_bytes=40 * 2**20),
+            compiler_params=pltpu.CompilerParams(vmem_limit_bytes=grant * 2**20),
             cost_estimate=pl.CostEstimate(flops=flops, bytes_accessed=moved, transcendentals=0),
         )
 
     def exchange(blocks, axes):
         return lax.all_to_all(blocks, axes, 0, 0, tiled=True)
 
-    def to_all(block, axes, count):
-        return exchange(jnp.broadcast_to(block[None], (count,) + block.shape), axes)
+    def to_all(block, axes):
+        return exchange(jnp.broadcast_to(block[None], (count(axes),) + block.shape), axes)
 
     def body(latent_in, out_grad, q_prev):
         rows, width, cout = out_grad.shape[1:]
@@ -159,31 +168,35 @@
         pixels = rows * width
         x = latent_in.reshape(-1, cin)
         g = out_grad.reshape(pixels, cout)
-        g_scratch = [pltpu.VMEM((pixels, cout), BF16), pltpu.SemaphoreType.DMA]
+        q_turned = jnp.swapaxes(q_prev, 1, 2)
+        loaded = [pltpu.VMEM(array.shape, BF16) for array in (x, q_turned, g)]
         whole_p = pltpu.VMEM((rank, cout), F32)
-        own = rank // n_plane
 
         p_term = call(
             lambda *refs: left_kernel(width, *refs),
-            jax.ShapeDtypeStruct((n_plane, own, cout), F32),
-            [VMEM, ANY, VMEM],
-            g_scratch,
+            jax.ShapeDtypeStruct((count(p_split), rank // count(p_split), cout), F32),
+            [HBM, HBM, HBM],
+            loaded + [pltpu.SemaphoreType.DMA((3,))],
             2 * pixels * cout * 256,
             2 * pixels * cout,
-        )(x, g, q_prev)
-        piece = jnp.sum(exchange(p_term, planes), axis=0)
-        piece = jnp.sum(to_all(piece, "z", n_z), axis=0)
-        p_pieces = to_all(piece, planes, n_plane)
+            grant=60,
+        )(x, q_turned, g)
+        piece = jnp.sum(exchange(p_term, p_split), axis=0)
+        piece, x_again, g_again = lax.optimization_barrier((piece, x, g))
+        piece = jnp.sum(to_all(piece, rest), axis=0)
+        p_pieces = to_all(piece, p_split)
 
         q_term = call(
             lambda *refs: right_kernel(width, *refs),
-            jax.ShapeDtypeStruct((n_x, rank // n_x, taps * cin), F32),
-            [VMEM, VMEM, ANY],
-            [whole_p] + g_scratch,
+            jax.ShapeDtypeStruct((count(q_split), rank // count(q_split), taps * cin), F32),
+            [VMEM, VMEM, VMEM],
+            [whole_p],
             4 * pixels * cout * 256,
             2 * pixels * cout,
-        )(p_pieces, x, g)
-
+        )(p_pieces, x_again, g_again)
+
+        part = jnp.sum(exchange(q_term, q_split), axis=0)
+        part, p_again = lax.optimization_barrier((part, p_pieces))
         inverse, p_whole = call(
             lambda *refs: factor_kernel(math.sqrt(cout), *refs),
             (jax.ShapeDtypeStruct((rank, rank), F32), jax.ShapeDtypeStruct((cout, rank), F32)),
@@ -191,28 +204,24 @@
             [whole_p],
             2 * pixels * cout * 256,
             2 * pixels * cout,
-        )(p_pieces)
-        share = cout // (n_x * n_z)
-        at = (lax.axis_index("x") * n_z + lax.axis_index("z")) * share
+        )(p_again)
+        share = cout // count(sample)
+        at = lax.axis_index(sample) * share
         p_factor = lax.dynamic_slice_in_dim(p_whole, at, share, axis=0)
-
-        part = jnp.sum(exchange(q_term, "x"), axis=0)
-        part = part.reshape(n_z, rank // (n_x * n_z), taps * cin)
-        part = jnp.sum(exchange(part, "z"), axis=0)
-        part = to_all(part, "z", n_z).reshape(rank // n_x, taps * cin)
-        q_raw = to_all(part, "x", n_x)
+        part = jnp.sum(to_all(part, rest), axis=0)
+        part, inverse, p_factor = lax.optimization_barrier((part, inverse, p_factor))
+        q_raw = to_all(part, q_split)
 
         q_factor = call(
             lambda *refs: finish_kernel(1.0 / math.sqrt(cout), *refs),
-            jax.ShapeDtypeStruct((taps * cin, rank), F32),
+            jax.ShapeDtypeStruct((taps, rank, cin), F32),
             [VMEM, VMEM],
             [],
             2 * taps * cin * rank * 256,
             8 * taps * cin * rank,
         )(q_raw, inverse)
-        return p_factor, q_factor.reshape(taps, cin, rank)
-
-    sample, channel = ("x", "z"), ("y", "c")
+        return p_factor, jnp.swapaxes(q_factor, 1, 2)
+
     return jax.shard_map(
         body,
         mesh=grid,

time: 130 us -> 122 us (0.938)
  the two profiles are of different devices: /device:TPU:2 before, /device:TPU:64 now
where the time goes in v2:
time: 122 us; the launch traced here: 121 us
  blocking collectives  82.1 us (67%)
  waiting for transfers between devices  16.9 us (14%)
  Pallas kernels  13.7 us (11%)
  starting transfers between devices  5.71 us (5%)
  local copies, waits for them, and re-layouts  1.62 us (1%)
    all_to_all x5, blocking collectives, exchange(): return lax.all_to_all(blocks, axes, 0, 0, tiled=True)  82.1 us
    all_to_all x1, waiting for transfers between devices, exchange(): return lax.all_to_all(blocks, axes, 0, 0, tiled=True)  16.9 us
    pallas_call x1, Pallas kernels, body(): call(lambda *refs: factor_kernel(math.sqrt(cout), *refs), (jax.ShapeDtype...  6.75 us
    all_to_all x1, starting transfers between devices, exchange(): return lax.all_to_all(blocks, axes, 0, 0, tiled=True)  5.71 us
    pallas_call x1, Pallas kernels, body(): call(lambda *refs: left_kernel(width, *refs), jax.ShapeDtypeStruct((count...  3.66 us
  transfers between devices with their start and end apart: 1, of which 1 were waited for; matrix products, arithmetic and copies ran while one was open for 1% of the time, Pallas kernels for 6%

profile of v2, /device:TPU:64, one launch (start us, length us, event | category | flops | bytes accessed | tf_op | source)
XLA Modules:
  0.0 121.1 jit_solution(7098726988804756844)
XLA Ops:
  0.6 0.0 copy-start
  0.6 0.0 copy-start.1
  0.6 3.7 %shard_map.50 = f32[64,1,1280]{2,1,0:T(1,128)} custom-call(bf16[1088,160]{1,0:T(8,128)(2,1)} %bitcast.6, bf16[9,64,160]{2,1,0:T(8,128)(2,1)} %bitcast.9, bf16[1024,1280]{1,0:T(8,128)(2,1)} %bitcast.4), custom_call_target="tpu_custom_call" | custom-call | flops 671088640 | bytes 2621440 | tf_op jit(solution)/shard_map/pallas_call | solution.py:175
  4.3 19.7 %all_to_all.30 = f32[64,1,1280]{2,1,0:T(1,128)S(1)} all-to-all(f32[64,1,1280]{2,1,0:T(1,128)} %shard_map.50), channel_id=1, replica_groups=mesh['x'=4,'far'=8,'near'=2,'y'=4,'c'=2] {'x','near','y','c'}, dimensions={0} | all-to-all | bytes 655360 | tf_op jit(solution)/shard_map/all_to_all | solution.py:160
  24.0 0.2 reduce_sum.38
  24.3 24.2 %all_to_all.31 = f32[8,1,1280]{2,1,0:T(1,128)S(1)} all-to-all(f32[8,1,1280]{2,1,0:T(1,128)S(1)} %broadcast_in_dim.11), channel_id=1, replica_groups=mesh['x'=4,'far'=8,'near'=2,'y'=4,'c'=2] {'far'}, dimensions={0} | all-to-all | bytes 81920 | tf_op jit(solution)/shard_map/all_to_all | solution.py:160
  48.5 0.2 broadcast_in_dim.12
  48.7 14.9 %all_to_all.32.refs_0_ = f32[64,1,1280]{2,1,0:T(1,128)S(1)} all-to-all(f32[64,1,1280]{2,1,0:T(1,128)S(1)} %broadcast_in_dim.12), channel_id=1, replica_groups=mesh['x'=4,'far'=8,'near'=2,'y'=4,'c'=2] {'x','near','y','c'}, dimensions={0} | all-to-all | bytes 655360 | tf_op jit(solution)/shard_map/all_to_all | solution.py:160
  63.7 0.0 copy-done
  63.7 0.0 copy-done.1
  63.7 2.1 %shard_map.51 = f32[8,8,1440]{2,1,0:T(8,128)S(1)} custom-call(f32[64,1,1280]{2,1,0:T(1,128)S(1)} %all_to_all.32.refs_0_, bf16[1088,160]{1,0:T(8,128)(2,1)S(1)} %bitcast.7, bf16[1024,1280]{1,0:T(8,128)(2,1)S(1)} %bitcast.5), custom_call_target="tpu_custom_call" | custom-call | flops 1342177280 | bytes 2621440 | tf_op jit(solution)/shard_map/pallas_call | solution.py:189
  65.8 11.7 %all_to_all.33 = f32[8,8,1440]{2,1,0:T(8,128)S(1)} all-to-all(f32[8,8,1440]{2,1,0:T(8,128)S(1)} %shard_map.51), channel_id=1, replica_groups=mesh['x'=4,'far'=8,'near'=2,'y'=4,'c'=2] {'x','near'}, dimensions={0} | all-to-all | bytes 737280 | tf_op jit(solution)/shard_map/all_to_all | solution.py:160
  77.6 0.8 broadcast_in_dim.13
  78.4 5.7 %all-to-all-start.4 = ((f32[8,8,1440]{2,1,0:T(8,128)}), f32[8,8,1440]{2,1,0:T(8,128)S(1)}, u32[]{:S(2)}, u32[]{:S(2)}) async-start(f32[8,8,1440]{2,1,0:T(8,128)} %broadcast_in_dim.13), calls=%async_computation.4 | async-start | bytes 786432 | tf_op jit(solution)/shard_map/all_to_all | solution.py:160
  84.1 6.8 %shard_map.52 = (f32[64,64]{1,0:T(8,128)S(1)}, f32[1280,64]{1,0:T(8,128)S(1)}) custom-call(f32[64,1,1280]{2,1,0:T(1,128)S(1)} %all_to_all.32.refs_0_), custom_call_target="tpu_custom_call" | custom-call | flops 671088640 | bytes 2621440 | tf_op jit(solution)/shard_map/pallas_call | solution.py:200
  90.8 0.6 constant_dynamic-slice_fusion
  91.4 16.9 %all-to-all-done.4 = f32[8,8,1440]{2,1,0:T(8,128)S(1)} async-done(((f32[8,8,1440]{2,1,0:T(8,128)}), f32[8,8,1440]{2,1,0:T(8,128)S(1)}, u32[]{:S(2)}, u32[]{:S(2)}) %all-to-all-start.4) | async-done | bytes 368672 | tf_op jit(solution)/shard_map/all_to_all | solution.py:160
  108.4 11.5 %all_to_all.34.refs_0_ = f32[8,8,1440]{2,1,0:T(8,128)S(1)} all-to-all(f32[8,8,1440]{2,1,0:T(8,128)S(1)} %broadcast_in_dim.14), channel_id=1, replica_groups=mesh['x'=4,'far'=8,'near'=2,'y'=4,'c'=2] {'x','near'}, dimensions={0} | all-to-all | bytes 737280 | tf_op jit(solution)/shard_map/all_to_all | solution.py:160
  119.9 1.2 shard_map.53
  (7 shorter events, 0.2 us)
Async XLA Ops:
  0.6 63.0 %copy-start = (bf16[1,32,32,1280]{3,2,1,0:T(8,128)(2,1)S(1)}, bf16[1,32,32,1280]{3,2,1,0:T(8,128)(2,1)}, u32[]{:S(2)}) copy-start(bf16[1,32,32,1280]{3,2,1,0:T(8,128)(2,1)} %param.4) | copy-start | bytes 7864324
  0.6 63.0 %copy-start.1 = (bf16[1,34,32,160]{3,2,1,0:T(8,128)(2,1)S(1)}, bf16[1,34,32,160]{3,2,1,0:T(8,128)(2,1)}, u32[]{:S(2)}) copy-start(bf16[1,34,32,160]{3,2,1,0:T(8,128)(2,1)} %param.3) | copy-start | bytes 1044484
  78.4 30.0 %all-to-all-start.4 = ((f32[8,8,1440]{2,1,0:T(8,128)}), f32[8,8,1440]{2,1,0:T(8,128)S(1)}, u32[]{:S(2)}, u32[]{:S(2)}) async-start(f32[8,8,1440]{2,1,0:T(8,128)} %broadcast_in_dim.13), calls=%async_computation.4 | async-start | bytes 786432 | tf_op jit(solution)/shard_map/all_to_all | solution.py:160

commit v3 on v2

--- a/solution.py
+++ b/solution.py
@@ -1,3 +1,4 @@
+import itertools
 import math
 
 import jax
@@ -26,7 +27,7 @@
     return lax.dot_general(left, right, (dims, ((), ())), preferred_element_type=F32)
 
 
-def left_kernel(width, x_hbm, q_hbm, g_hbm, out_ref, x_ref, q_ref, g_ref, sems):
+def left_kernel(width, x_hbm, q_hbm, g_hbm, out_ref, x_ref, g_ref, q_ref, sems):
     loads = [
         pltpu.make_async_copy(source, target, sems.at[i])
         for i, (source, target) in enumerate(((x_hbm, x_ref), (q_hbm, q_ref), (g_hbm, g_ref)))
@@ -136,14 +137,17 @@
 
 
 def solution(mesh):
-    sizes = {"x": 4, "far": 8, "near": 2, "y": 4, "c": 2}
+    sizes = {"x": 4, "far": 4, "middle": 2, "near": 2, "y": 4, "c": 2}
     grid = Mesh(mesh.devices.reshape(tuple(sizes.values())), tuple(sizes))
 
     def count(axes):
         return math.prod(sizes[axis] for axis in axes)
 
-    sample, channel = ("x", "far", "near"), ("y", "c")
-    p_split, q_split, rest = ("x", "near", "y", "c"), ("x", "near"), ("far",)
+    sample, channel = ("x", "far", "middle", "near"), ("y", "c")
+    p_split, p_rest = ("x", "near", "y", "c"), ("far", "middle")
+    q_split, q_rest = ("x", "middle", "near"), ("far",)
+
+    first = {"far": 2, "x": 2, "y": 2, "near": 1}
 
     def call(kernel, out_shape, in_specs, scratch, flops, moved, grant=40):
         return pl.pallas_call(
@@ -156,7 +160,27 @@
             cost_estimate=pl.CostEstimate(flops=flops, bytes_accessed=moved, transcendentals=0),
         )
 
+    def groups_of(axes):
+        others = [axis for axis in sizes if axis not in axes]
+        groups = []
+        for place in itertools.product(*(range(sizes[axis]) for axis in others)):
+            group = []
+            for steps in itertools.product(*(range(sizes[axis]) for axis in axes)):
+                at = dict(zip(others, place))
+                for axis, step in zip(axes, steps):
+                    at[axis] = (step + first.get(axis, 0)) % sizes[axis]
+                index = 0
+                for axis, size in sizes.items():
+                    index = index * size + at[axis]
+                group.append(index)
+            groups.append(group)
+        return groups
+
     def exchange(blocks, axes):
+        if any(axis in first for axis in axes):
+            return lax.all_to_all(
+                blocks, tuple(sizes), 0, 0, tiled=True, axis_index_groups=groups_of(axes)
+            )
         return lax.all_to_all(blocks, axes, 0, 0, tiled=True)
 
     def to_all(block, axes):
@@ -169,21 +193,23 @@
         x = latent_in.reshape(-1, cin)
         g = out_grad.reshape(pixels, cout)
         q_turned = jnp.swapaxes(q_prev, 1, 2)
-        loaded = [pltpu.VMEM(array.shape, BF16) for array in (x, q_turned, g)]
         whole_p = pltpu.VMEM((rank, cout), F32)
 
-        p_term = call(
+        p_term, x_held, g_held = call(
             lambda *refs: left_kernel(width, *refs),
-            jax.ShapeDtypeStruct((count(p_split), rank // count(p_split), cout), F32),
+            (
+                jax.ShapeDtypeStruct((count(p_split), rank // count(p_split), cout), F32),
+                jax.ShapeDtypeStruct(x.shape, BF16),
+                jax.ShapeDtypeStruct(g.shape, BF16),
+            ),
             [HBM, HBM, HBM],
-            loaded + [pltpu.SemaphoreType.DMA((3,))],
+            [pltpu.VMEM(q_turned.shape, BF16), pltpu.SemaphoreType.DMA((3,))],
             2 * pixels * cout * 256,
             2 * pixels * cout,
-            grant=60,
-        )(x, q_turned, g)
+            grant=16,
+        )(*(pltpu.with_memory_space_constraint(array, pltpu.HBM) for array in (x, q_turned, g)))
         piece = jnp.sum(exchange(p_term, p_split), axis=0)
-        piece, x_again, g_again = lax.optimization_barrier((piece, x, g))
-        piece = jnp.sum(to_all(piece, rest), axis=0)
+        piece = jnp.sum(to_all(piece, p_rest), axis=0)
         p_pieces = to_all(piece, p_split)
 
         q_term = call(
@@ -193,10 +219,9 @@
             [whole_p],
             4 * pixels * cout * 256,
             2 * pixels * cout,
-        )(p_pieces, x_again, g_again)
+        )(p_pieces, x_held, g_held)
 
         part = jnp.sum(exchange(q_term, q_split), axis=0)
-        part, p_again = lax.optimization_barrier((part, p_pieces))
         inverse, p_whole = call(
             lambda *refs: factor_kernel(math.sqrt(cout), *refs),
             (jax.ShapeDtypeStruct((rank, rank), F32), jax.ShapeDtypeStruct((cout, rank), F32)),
@@ -204,12 +229,12 @@
             [whole_p],
             2 * pixels * cout * 256,
             2 * pixels * cout,
-        )(p_again)
+        )(p_pieces)
         share = cout // count(sample)
         at = lax.axis_index(sample) * share
         p_factor = lax.dynamic_slice_in_dim(p_whole, at, share, axis=0)
-        part = jnp.sum(to_all(part, rest), axis=0)
         part, inverse, p_factor = lax.optimization_barrier((part, inverse, p_factor))
+        part = jnp.sum(to_all(part, q_rest), axis=0)
         q_raw = to_all(part, q_split)
 
         q_factor = call(

time: 122 us -> 107 us (0.88)
  the two profiles are of different devices: /device:TPU:64 before, /device:TPU:2 now
where the time goes in v3:
time: 107 us
  blocking collectives  80 us (75%)
  Pallas kernels  13.7 us (13%)
  starting transfers between devices  6.65 us (6%)
  waiting for transfers between devices  4.47 us (4%)
    all_to_all x5, blocking collectives, exchange(): lax.all_to_all(blocks, tuple(sizes), 0, 0, tiled=True, axis_index_groups=...  80 us
    pallas_call x1, Pallas kernels, body(): call(lambda *refs: factor_kernel(math.sqrt(cout), *refs), (jax.ShapeDtype...  6.75 us
    all_to_all x1, starting transfers between devices, exchange(): lax.all_to_all(blocks, tuple(sizes), 0, 0, tiled=True, axis_index_groups=...  6.65 us
    all_to_all x1, waiting for transfers between devices, exchange(): lax.all_to_all(blocks, tuple(sizes), 0, 0, tiled=True, axis_index_groups=...  4.47 us
    pallas_call x1, Pallas kernels, body(): call(lambda *refs: right_kernel(width, *refs), jax.ShapeDtypeStruct((coun...  2.89 us
    pallas_call x1, Pallas kernels, body(): call(lambda *refs: left_kernel(width, *refs), (jax.ShapeDtypeStruct((coun...  2.81 us
  transfers between devices with their start and end apart: 1, of which 1 were waited for; matrix products, arithmetic and copies ran while one was open for 1% of the time, Pallas kernels for 6%

profile of v3, /device:TPU:2, one launch (start us, length us, event | category | flops | bytes accessed | tf_op | source)
XLA Modules:
  0.0 106.7 jit_solution(9088310402597095671)
XLA Ops:
  0.6 2.8 %shard_map.50 = (f32[64,1,1280]{2,1,0:T(1,128)S(1)}, bf16[1088,160]{1,0:T(8,128)(2,1)S(1)}, bf16[1024,1280]{1,0:T(8,128)(2,1)S(1)}) custom-call(bf16[1088,160]{1,0:T(8,128)(2,1)} %bitcast.6, bf16[9,64,160]{2,1,0:T(8,128)(2,1)} %bitcast.7, bf16[1024,1280]{1,0:T(8,128)(2,1)} %bitcast.4), custom_call_target="tpu_custom_call" | custom-call | flops 671088640 | bytes 2621440 | tf_op jit(solution)/shard_map/pallas_call | solution.py:198
  3.5 18.7 %all_to_all.30 = f32[64,1,1280]{2,1,0:T(1,128)S(1)} all-to-all(f32[64,1,1280]{2,1,0:T(1,128)S(1)} %get-tuple-element.10), channel_id=1, replica_groups={{268,269,270,271,264,265,266,267,260,261,262,263,256,257,258,259,396,39..., dimensions={0} | all-to-all | bytes 655360 | tf_op jit(solution)/shard_map/all_to_all | solution.py:181
  22.1 0.2 reduce_sum.36
  22.4 17.2 %all_to_all.31 = f32[8,1,1280]{2,1,0:T(1,128)S(1)} all-to-all(f32[8,1,1280]{2,1,0:T(1,128)S(1)} %broadcast_in_dim.8), channel_id=1, replica_groups={{64,80,96,112,0,16,32,48},{65,81,97,113,1,17,33,49},{66,82,98,114,2,18,..., dimensions={0} | all-to-all | bytes 81920 | tf_op jit(solution)/shard_map/all_to_all | solution.py:181
  39.6 0.2 broadcast_in_dim.9
  39.8 14.5 %all_to_all.32.refs_0_ = f32[64,1,1280]{2,1,0:T(1,128)S(1)} all-to-all(f32[64,1,1280]{2,1,0:T(1,128)S(1)} %broadcast_in_dim.9), channel_id=1, replica_groups={{268,269,270,271,264,265,266,267,260,261,262,263,256,257,258,259,396,39..., dimensions={0} | all-to-all | bytes 655360 | tf_op jit(solution)/shard_map/all_to_all | solution.py:181
  54.3 2.9 %shard_map.51 = f32[16,4,1440]{2,1,0:T(4,128)} custom-call(f32[64,1,1280]{2,1,0:T(1,128)S(1)} %all_to_all.32.refs_0_, bf16[1088,160]{1,0:T(8,128)(2,1)S(1)} %get-tuple-element.11.refs_1_, bf16[1024,1280]{1,0:T(8,128)(2,1)S(1)} %get-tuple-element.12.refs_2_), custom_call_target="tpu_custom_call" | custom-call | flops 1342177280 | bytes 2621440 | tf_op jit(solution)/shard_map/pallas_call | solution.py:215
  57.2 6.6 %all-to-all-start.3 = ((f32[16,4,1440]{2,1,0:T(4,128)}), f32[16,4,1440]{2,1,0:T(4,128)S(1)}, u32[]{:S(2)}, u32[]{:S(2)}) async-start(f32[16,4,1440]{2,1,0:T(4,128)} %shard_map.51), calls=%async_computation.3 | async-start | bytes 786432 | tf_op jit(solution)/shard_map/all_to_all | solution.py:181
  63.8 6.8 %shard_map.52 = (f32[64,64]{1,0:T(8,128)S(1)}, f32[1280,64]{1,0:T(8,128)S(1)}) custom-call(f32[64,1,1280]{2,1,0:T(1,128)S(1)} %all_to_all.32.refs_0_), custom_call_target="tpu_custom_call" | custom-call | flops 671088640 | bytes 2621440 | tf_op jit(solution)/shard_map/pallas_call | solution.py:225
  70.6 0.6 constant_dynamic-slice_fusion
  71.2 4.5 %all-to-all-done.3 = f32[16,4,1440]{2,1,0:T(4,128)S(1)} async-done(((f32[16,4,1440]{2,1,0:T(4,128)}), f32[16,4,1440]{2,1,0:T(4,128)S(1)}, u32[]{:S(2)}, u32[]{:S(2)}) %all-to-all-start.3) | async-done | bytes 368672 | tf_op jit(solution)/shard_map/all_to_all | solution.py:181
  75.7 0.1 reduce_sum.38
  75.8 15.4 %all_to_all.33 = f32[4,4,1440]{2,1,0:T(4,128)S(1)} all-to-all(f32[4,4,1440]{2,1,0:T(4,128)S(1)} %broadcast_in_dim.10), channel_id=1, replica_groups={{64,96,0,32},{65,97,1,33},{66,98,2,34},{67,99,3,35},{68,100,4,36},{69,1..., dimensions={0} | all-to-all | bytes 184320 | tf_op jit(solution)/shard_map/all_to_all | solution.py:181
  91.2 0.1 broadcast_in_dim.11
  91.2 14.2 %all_to_all.34.refs_0_ = f32[16,4,1440]{2,1,0:T(4,128)S(1)} all-to-all(f32[16,4,1440]{2,1,0:T(4,128)S(1)} %broadcast_in_dim.11), channel_id=1, replica_groups={{264,256,280,272,392,384,408,400,8,0,24,16,136,128,152,144},{265,257,28..., dimensions={0} | all-to-all | bytes 737280 | tf_op jit(solution)/shard_map/all_to_all | solution.py:181
  105.5 1.2 %shard_map.53 = f32[9,64,160]{2,1,0:T(8,128)} custom-call(f32[16,4,1440]{2,1,0:T(4,128)S(1)} %all_to_all.34.refs_0_, f32[64,64]{1,0:T(8,128)S(1)} %get-tuple-element.17.refs_1_), custom_call_target="tpu_custom_call" | custom-call | flops 47185920 | bytes 737280 | tf_op jit(solution)/shard_map/pallas_call | solution.py:240
  (4 shorter events, 0.1 us)
Async XLA Ops:
  57.2 18.5 %all-to-all-start.3 = ((f32[16,4,1440]{2,1,0:T(4,128)}), f32[16,4,1440]{2,1,0:T(4,128)S(1)}, u32[]{:S(2)}, u32[]{:S(2)}) async-start(f32[16,4,1440]{2,1,0:T(4,128)} %shard_map.51), calls=%async_computation.3 | async-start | bytes 786432 | tf_op jit(solution)/shard_map/all_to_all | solution.py:181

commit v4 on v3

--- a/solution.py
+++ b/solution.py
@@ -147,7 +147,8 @@
     p_split, p_rest = ("x", "near", "y", "c"), ("far", "middle")
     q_split, q_rest = ("x", "middle", "near"), ("far",)
 
-    first = {"far": 2, "x": 2, "y": 2, "near": 1}
+    p_first, far_first = {"x": 2, "y": 2, "near": 1}, {"far": 2, "middle": 1}
+    q_first, last_first = {"x": 2, "middle": 1}, {"far": 2}
 
     def call(kernel, out_shape, in_specs, scratch, flops, moved, grant=40):
         return pl.pallas_call(
@@ -160,7 +161,7 @@
             cost_estimate=pl.CostEstimate(flops=flops, bytes_accessed=moved, transcendentals=0),
         )
 
-    def groups_of(axes):
+    def groups_of(axes, first):
         others = [axis for axis in sizes if axis not in axes]
         groups = []
         for place in itertools.product(*(range(sizes[axis]) for axis in others)):
@@ -176,15 +177,15 @@
             groups.append(group)
         return groups
 
-    def exchange(blocks, axes):
+    def exchange(blocks, axes, first):
         if any(axis in first for axis in axes):
             return lax.all_to_all(
-                blocks, tuple(sizes), 0, 0, tiled=True, axis_index_groups=groups_of(axes)
+                blocks, tuple(sizes), 0, 0, tiled=True, axis_index_groups=groups_of(axes, first)
             )
         return lax.all_to_all(blocks, axes, 0, 0, tiled=True)
 
-    def to_all(block, axes):
-        return exchange(jnp.broadcast_to(block[None], (count(axes),) + block.shape), axes)
+    def to_all(block, axes, first):
+        return exchange(jnp.broadcast_to(block[None], (count(axes),) + block.shape), axes, first)
 
     def body(latent_in, out_grad, q_prev):
         rows, width, cout = out_grad.shape[1:]
@@ -208,9 +209,9 @@
             2 * pixels * cout,
             grant=16,
         )(*(pltpu.with_memory_space_constraint(array, pltpu.HBM) for array in (x, q_turned, g)))
-        piece = jnp.sum(exchange(p_term, p_split), axis=0)
-        piece = jnp.sum(to_all(piece, p_rest), axis=0)
-        p_pieces = to_all(piece, p_split)
+        piece = jnp.sum(exchange(p_term, p_split, p_first), axis=0)
+        piece = jnp.sum(to_all(piece, p_rest, far_first), axis=0)
+        p_pieces = to_all(piece, p_split, p_first)
 
         q_term = call(
             lambda *refs: right_kernel(width, *refs),
@@ -221,7 +222,7 @@
             2 * pixels * cout,
         )(p_pieces, x_held, g_held)
 
-        part = jnp.sum(exchange(q_term, q_split), axis=0)
+        part = jnp.sum(exchange(q_term, q_split, q_first), axis=0)
         inverse, p_whole = call(
             lambda *refs: factor_kernel(math.sqrt(cout), *refs),
             (jax.ShapeDtypeStruct((rank, rank), F32), jax.ShapeDtypeStruct((cout, rank), F32)),
@@ -234,8 +235,8 @@
         at = lax.axis_index(sample) * share
         p_factor = lax.dynamic_slice_in_dim(p_whole, at, share, axis=0)
         part, inverse, p_factor = lax.optimization_barrier((part, inverse, p_factor))
-        part = jnp.sum(to_all(part, q_rest), axis=0)
-        q_raw = to_all(part, q_split)
+        part = jnp.sum(to_all(part, q_rest, last_first), axis=0)
+        q_raw = to_all(part, q_split, q_first)
 
         q_factor = call(
             lambda *refs: finish_kernel(1.0 / math.sqrt(cout), *refs),

time: 107 us -> 105 us (0.981)
  the two profiles are of different devices: /device:TPU:2 before, /device:TPU:8 now
where the time goes in v4:
time: 105 us
  blocking collectives  80 us (76%)
  Pallas kernels  13.6 us (13%)
  starting transfers between devices  7.16 us (7%)
  waiting for transfers between devices  2.23 us (2%)
    all_to_all x5, blocking collectives, exchange(): lax.all_to_all(blocks, tuple(sizes), 0, 0, tiled=True, axis_index_groups=...  80 us
    all_to_all x1, starting transfers between devices, exchange(): lax.all_to_all(blocks, tuple(sizes), 0, 0, tiled=True, axis_index_groups=...  7.16 us
    pallas_call x1, Pallas kernels, body(): call(lambda *refs: factor_kernel(math.sqrt(cout), *refs), (jax.ShapeDtype...  6.75 us
    pallas_call x1, Pallas kernels, body(): call(lambda *refs: right_kernel(width, *refs), jax.ShapeDtypeStruct((coun...  2.89 us
    pallas_call x1, Pallas kernels, body(): call(lambda *refs: left_kernel(width, *refs), (jax.ShapeDtypeStruct((coun...  2.81 us
    all_to_all x1, waiting for transfers between devices, exchange(): lax.all_to_all(blocks, tuple(sizes), 0, 0, tiled=True, axis_index_groups=...  2.23 us
  transfers between devices with their start and end apart: 1, of which 1 were waited for; matrix products, arithmetic and copies ran while one was open for 1% of the time, Pallas kernels for 6%

profile of v4, /device:TPU:8, one launch (start us, length us, event | category | flops | bytes accessed | tf_op | source)
XLA Modules:
  0.0 104.9 jit_solution(16709533536264553534)
XLA Ops:
  0.6 2.8 %shard_map.50 = (f32[64,1,1280]{2,1,0:T(1,128)S(1)}, bf16[1088,160]{1,0:T(8,128)(2,1)S(1)}, bf16[1024,1280]{1,0:T(8,128)(2,1)S(1)}) custom-call(bf16[1088,160]{1,0:T(8,128)(2,1)} %bitcast.6, bf16[9,64,160]{2,1,0:T(8,128)(2,1)} %bitcast.7, bf16[1024,1280]{1,0:T(8,128)(2,1)} %bitcast.4), custom_call_target="tpu_custom_call" | custom-call | flops 671088640 | bytes 2621440 | tf_op jit(solution)/shard_map/pallas_call | solution.py:199
  3.4 18.6 %all_to_all.30 = f32[64,1,1280]{2,1,0:T(1,128)S(1)} all-to-all(f32[64,1,1280]{2,1,0:T(1,128)S(1)} %get-tuple-element.10), channel_id=1, replica_groups={{268,269,270,271,264,265,266,267,260,261,262,263,256,257,258,259,396,39..., dimensions={0} | all-to-all | bytes 655360 | tf_op jit(solution)/shard_map/all_to_all | solution.py:182
  22.0 0.2 reduce_sum.36
  22.2 17.1 %all_to_all.31 = f32[8,1,1280]{2,1,0:T(1,128)S(1)} all-to-all(f32[8,1,1280]{2,1,0:T(1,128)S(1)} %broadcast_in_dim.8), channel_id=1, replica_groups={{80,64,112,96,16,0,48,32},{81,65,113,97,17,1,49,33},{82,66,114,98,18,2,..., dimensions={0} | all-to-all | bytes 81920 | tf_op jit(solution)/shard_map/all_to_all | solution.py:182
  39.4 0.2 broadcast_in_dim.9
  39.5 14.8 %all_to_all.32.refs_0_ = f32[64,1,1280]{2,1,0:T(1,128)S(1)} all-to-all(f32[64,1,1280]{2,1,0:T(1,128)S(1)} %broadcast_in_dim.9), channel_id=1, replica_groups={{268,269,270,271,264,265,266,267,260,261,262,263,256,257,258,259,396,39..., dimensions={0} | all-to-all | bytes 655360 | tf_op jit(solution)/shard_map/all_to_all | solution.py:182
  54.4 2.9 %shard_map.51 = f32[16,4,1440]{2,1,0:T(4,128)} custom-call(f32[64,1,1280]{2,1,0:T(1,128)S(1)} %all_to_all.32.refs_0_, bf16[1088,160]{1,0:T(8,128)(2,1)S(1)} %get-tuple-element.11.refs_1_, bf16[1024,1280]{1,0:T(8,128)(2,1)S(1)} %get-tuple-element.12.refs_2_), custom_call_target="tpu_custom_call" | custom-call | flops 1342177280 | bytes 2621440 | tf_op jit(solution)/shard_map/pallas_call | solution.py:216
  57.3 7.2 %all-to-all-start.3 = ((f32[16,4,1440]{2,1,0:T(4,128)}), f32[16,4,1440]{2,1,0:T(4,128)S(1)}, u32[]{:S(2)}, u32[]{:S(2)}) async-start(f32[16,4,1440]{2,1,0:T(4,128)} %shard_map.51), calls=%async_computation.3 | async-start | bytes 786432 | tf_op jit(solution)/shard_map/all_to_all | solution.py:182
  64.4 6.8 %shard_map.52 = (f32[64,64]{1,0:T(8,128)S(1)}, f32[1280,64]{1,0:T(8,128)S(1)}) custom-call(f32[64,1,1280]{2,1,0:T(1,128)S(1)} %all_to_all.32.refs_0_), custom_call_target="tpu_custom_call" | custom-call | flops 671088640 | bytes 2621440 | tf_op jit(solution)/shard_map/pallas_call | solution.py:226
  71.2 0.6 constant_dynamic-slice_fusion
  71.8 2.2 %all-to-all-done.3 = f32[16,4,1440]{2,1,0:T(4,128)S(1)} async-done(((f32[16,4,1440]{2,1,0:T(4,128)}), f32[16,4,1440]{2,1,0:T(4,128)S(1)}, u32[]{:S(2)}, u32[]{:S(2)}) %all-to-all-start.3) | async-done | bytes 368672 | tf_op jit(solution)/shard_map/all_to_all | solution.py:182
  74.0 0.1 reduce_sum.38
  74.1 15.4 %all_to_all.33 = f32[4,4,1440]{2,1,0:T(4,128)S(1)} all-to-all(f32[4,4,1440]{2,1,0:T(4,128)S(1)} %broadcast_in_dim.10), channel_id=1, replica_groups={{64,96,0,32},{65,97,1,33},{66,98,2,34},{67,99,3,35},{68,100,4,36},{69,1..., dimensions={0} | all-to-all | bytes 184320 | tf_op jit(solution)/shard_map/all_to_all | solution.py:182
  89.6 0.1 broadcast_in_dim.11
  89.6 14.1 %all_to_all.34.refs_0_ = f32[16,4,1440]{2,1,0:T(4,128)S(1)} all-to-all(f32[16,4,1440]{2,1,0:T(4,128)S(1)} %broadcast_in_dim.11), channel_id=1, replica_groups={{272,280,256,264,400,408,384,392,16,24,0,8,144,152,128,136},{273,281,25..., dimensions={0} | all-to-all | bytes 737280 | tf_op jit(solution)/shard_map/all_to_all | solution.py:182
  103.7 1.2 %shard_map.53 = f32[9,64,160]{2,1,0:T(8,128)} custom-call(f32[16,4,1440]{2,1,0:T(4,128)S(1)} %all_to_all.34.refs_0_, f32[64,64]{1,0:T(8,128)S(1)} %get-tuple-element.17.refs_1_), custom_call_target="tpu_custom_call" | custom-call | flops 47185920 | bytes 737280 | tf_op jit(solution)/shard_map/pallas_call | solution.py:241
  (4 shorter events, 0.1 us)
Async XLA Ops:
  57.3 16.8 %all-to-all-start.3 = ((f32[16,4,1440]{2,1,0:T(4,128)}), f32[16,4,1440]{2,1,0:T(4,128)S(1)}, u32[]{:S(2)}, u32[]{:S(2)}) async-start(f32[16,4,1440]{2,1,0:T(4,128)} %shard_map.51), calls=%async_computation.3 | async-start | bytes 786432 | tf_op jit(solution)/shard_map/all_to_all | solution.py:182

commit v5 on v4

--- a/solution.py
+++ b/solution.py
@@ -50,10 +50,10 @@
         + jnp.where(column == 0, 0.0, before)
         + jnp.where(column == width - 1, 0.0, after)
     )
-    stacked = jnp.concatenate(parts_of(projected), axis=0)
+    stacked = jnp.concatenate(parts_of(projected)[:2], axis=0)
     loads[2].wait()
     total = dot(stacked, g_ref[...], ((1,), (0,)))
-    total = total[:rank] + total[rank : 2 * rank] + total[2 * rank :]
+    total = total[:rank] + total[rank:]
     rows = out_ref.shape[1]
     for i in range(out_ref.shape[0]):
         out_ref[i] = total[rows * i : rows * (i + 1)]
@@ -68,21 +68,21 @@
 def right_kernel(width, p_ref, x_ref, g_ref, out_ref, whole_ref):
     gather_rows(p_ref, whole_ref)
     rank, pixels = whole_ref.shape[0], g_ref.shape[0]
-    stacked = jnp.concatenate(parts_of(whole_ref[...]), axis=0)
+    stacked = jnp.concatenate(parts_of(whole_ref[...])[:2], axis=0)
     mapped = dot(stacked, g_ref[...], ((1,), (1,)))
-    mapped = mapped[:rank] + mapped[rank : 2 * rank] + mapped[2 * rank :]
+    mapped = mapped[:rank] + mapped[rank:]
     column = lax.broadcasted_iota(jnp.int32, (rank, pixels), 1) & (width - 1)
     ahead = jnp.where(column == width - 1, 0.0, pltpu.roll(mapped, pixels - 1, 1))
     behind = jnp.where(column == 0, 0.0, pltpu.roll(mapped, 1, 1))
     shifted = jnp.concatenate(
-        [part for side in (ahead, mapped, behind) for part in parts_of(side)], axis=0
+        [part for side in (ahead, mapped, behind) for part in parts_of(side)[:2]], axis=0
     )
     pieces = []
     for a in range(3):
         term = dot(shifted, x_ref[width * a : width * a + pixels, :], ((1,), (0,)))
         for b in range(3):
-            t = term[3 * rank * b : 3 * rank * (b + 1)]
-            pieces.append(t[:rank] + t[rank : 2 * rank] + t[2 * rank :])
+            t = term[2 * rank * b : 2 * rank * (b + 1)]
+            pieces.append(t[:rank] + t[rank:])
     whole = jnp.concatenate(pieces, axis=1)
     groups, rows = out_ref.shape[0], out_ref.shape[1]
     for i in range(groups):

time: 105 us -> 105 us (level)
  no operation moved by 1% of the time
where the time goes in v5:
time: 105 us; the launch traced here: 104 us
  blocking collectives  80 us (76%)
  Pallas kernels  13.2 us (13%)
  starting transfers between devices  7.16 us (7%)
  waiting for transfers between devices  2.23 us (2%)
    all_to_all x5, blocking collectives, exchange(): lax.all_to_all(blocks, tuple(sizes), 0, 0, tiled=True, axis_index_groups=...  80 us
    all_to_all x1, starting transfers between devices, exchange(): lax.all_to_all(blocks, tuple(sizes), 0, 0, tiled=True, axis_index_groups=...  7.16 us
    pallas_call x1, Pallas kernels, body(): call(lambda *refs: factor_kernel(math.sqrt(cout), *refs), (jax.ShapeDtype...  6.75 us
    pallas_call x1, Pallas kernels, body(): call(lambda *refs: left_kernel(width, *refs), (jax.ShapeDtypeStruct((coun...  2.63 us
    pallas_call x1, Pallas kernels, body(): call(lambda *refs: right_kernel(width, *refs), jax.ShapeDtypeStruct((coun...  2.58 us
    all_to_all x1, waiting for transfers between devices, exchange(): lax.all_to_all(blocks, tuple(sizes), 0, 0, tiled=True, axis_index_groups=...  2.23 us
  transfers between devices with their start and end apart: 1, of which 1 were waited for; matrix products, arithmetic and copies ran while one was open for 1% of the time, Pallas kernels for 6%

profile of v5, /device:TPU:8, one launch (start us, length us, event | category | flops | bytes accessed | tf_op | source)
XLA Modules:
  0.0 104.4 jit_solution(8071723986400357391)
XLA Ops:
  0.6 2.6 %shard_map.50 = (f32[64,1,1280]{2,1,0:T(1,128)S(1)}, bf16[1088,160]{1,0:T(8,128)(2,1)S(1)}, bf16[1024,1280]{1,0:T(8,128)(2,1)S(1)}) custom-call(bf16[1088,160]{1,0:T(8,128)(2,1)} %bitcast.6, bf16[9,64,160]{2,1,0:T(8,128)(2,1)} %bitcast.7, bf16[1024,1280]{1,0:T(8,128)(2,1)} %bitcast.4), custom_call_target="tpu_custom_call" | custom-call | flops 671088640 | bytes 2621440 | tf_op jit(solution)/shard_map/pallas_call | solution.py:199
  3.3 18.6 %all_to_all.30 = f32[64,1,1280]{2,1,0:T(1,128)S(1)} all-to-all(f32[64,1,1280]{2,1,0:T(1,128)S(1)} %get-tuple-element.10), channel_id=1, replica_groups={{268,269,270,271,264,265,266,267,260,261,262,263,256,257,258,259,396,39..., dimensions={0} | all-to-all | bytes 655360 | tf_op jit(solution)/shard_map/all_to_all | solution.py:182
  21.8 0.2 reduce_sum.36
  22.1 17.1 %all_to_all.31 = f32[8,1,1280]{2,1,0:T(1,128)S(1)} all-to-all(f32[8,1,1280]{2,1,0:T(1,128)S(1)} %broadcast_in_dim.8), channel_id=1, replica_groups={{80,64,112,96,16,0,48,32},{81,65,113,97,17,1,49,33},{82,66,114,98,18,2,..., dimensions={0} | all-to-all | bytes 81920 | tf_op jit(solution)/shard_map/all_to_all | solution.py:182
  39.2 0.2 broadcast_in_dim.9
  39.4 14.8 %all_to_all.32.refs_0_ = f32[64,1,1280]{2,1,0:T(1,128)S(1)} all-to-all(f32[64,1,1280]{2,1,0:T(1,128)S(1)} %broadcast_in_dim.9), channel_id=1, replica_groups={{268,269,270,271,264,265,266,267,260,261,262,263,256,257,258,259,396,39..., dimensions={0} | all-to-all | bytes 655360 | tf_op jit(solution)/shard_map/all_to_all | solution.py:182
  54.2 2.6 %shard_map.51 = f32[16,4,1440]{2,1,0:T(4,128)} custom-call(f32[64,1,1280]{2,1,0:T(1,128)S(1)} %all_to_all.32.refs_0_, bf16[1088,160]{1,0:T(8,128)(2,1)S(1)} %get-tuple-element.11.refs_1_, bf16[1024,1280]{1,0:T(8,128)(2,1)S(1)} %get-tuple-element.12.refs_2_), custom_call_target="tpu_custom_call" | custom-call | flops 1342177280 | bytes 2621440 | tf_op jit(solution)/shard_map/pallas_call | solution.py:216
  56.8 7.2 %all-to-all-start.3 = ((f32[16,4,1440]{2,1,0:T(4,128)}), f32[16,4,1440]{2,1,0:T(4,128)S(1)}, u32[]{:S(2)}, u32[]{:S(2)}) async-start(f32[16,4,1440]{2,1,0:T(4,128)} %shard_map.51), calls=%async_computation.3 | async-start | bytes 786432 | tf_op jit(solution)/shard_map/all_to_all | solution.py:182
  63.9 6.8 %shard_map.52 = (f32[64,64]{1,0:T(8,128)S(1)}, f32[1280,64]{1,0:T(8,128)S(1)}) custom-call(f32[64,1,1280]{2,1,0:T(1,128)S(1)} %all_to_all.32.refs_0_), custom_call_target="tpu_custom_call" | custom-call | flops 671088640 | bytes 2621440 | tf_op jit(solution)/shard_map/pallas_call | solution.py:226
  70.7 0.6 constant_dynamic-slice_fusion
  71.3 2.2 %all-to-all-done.3 = f32[16,4,1440]{2,1,0:T(4,128)S(1)} async-done(((f32[16,4,1440]{2,1,0:T(4,128)}), f32[16,4,1440]{2,1,0:T(4,128)S(1)}, u32[]{:S(2)}, u32[]{:S(2)}) %all-to-all-start.3) | async-done | bytes 368672 | tf_op jit(solution)/shard_map/all_to_all | solution.py:182
  73.5 0.1 reduce_sum.38
  73.6 15.4 %all_to_all.33 = f32[4,4,1440]{2,1,0:T(4,128)S(1)} all-to-all(f32[4,4,1440]{2,1,0:T(4,128)S(1)} %broadcast_in_dim.10), channel_id=1, replica_groups={{64,96,0,32},{65,97,1,33},{66,98,2,34},{67,99,3,35},{68,100,4,36},{69,1..., dimensions={0} | all-to-all | bytes 184320 | tf_op jit(solution)/shard_map/all_to_all | solution.py:182
  89.1 0.1 broadcast_in_dim.11
  89.1 14.1 %all_to_all.34.refs_0_ = f32[16,4,1440]{2,1,0:T(4,128)S(1)} all-to-all(f32[16,4,1440]{2,1,0:T(4,128)S(1)} %broadcast_in_dim.11), channel_id=1, replica_groups={{272,280,256,264,400,408,384,392,16,24,0,8,144,152,128,136},{273,281,25..., dimensions={0} | all-to-all | bytes 737280 | tf_op jit(solution)/shard_map/all_to_all | solution.py:182
  103.2 1.2 %shard_map.53 = f32[9,64,160]{2,1,0:T(8,128)} custom-call(f32[16,4,1440]{2,1,0:T(4,128)S(1)} %all_to_all.34.refs_0_, f32[64,64]{1,0:T(8,128)S(1)} %get-tuple-element.17.refs_1_), custom_call_target="tpu_custom_call" | custom-call | flops 47185920 | bytes 737280 | tf_op jit(solution)/shard_map/pallas_call | solution.py:241
  (4 shorter events, 0.1 us)
Async XLA Ops:
  56.8 16.8 %all-to-all-start.3 = ((f32[16,4,1440]{2,1,0:T(4,128)}), f32[16,4,1440]{2,1,0:T(4,128)S(1)}, u32[]{:S(2)}, u32[]{:S(2)}) async-start(f32[16,4,1440]{2,1,0:T(4,128)} %shard_map.51), calls=%async_computation.3 | async-start | bytes 786432 | tf_op jit(solution)/shard_map/all_to_all | solution.py:182

commit v6 on v5

--- a/solution.py
+++ b/solution.py
@@ -147,7 +147,7 @@
     p_split, p_rest = ("x", "near", "y", "c"), ("far", "middle")
     q_split, q_rest = ("x", "middle", "near"), ("far",)
 
-    p_first, far_first = {"x": 2, "y": 2, "near": 1}, {"far": 2, "middle": 1}
+    p_first, far_first = {"x": 3, "y": 3, "near": 1}, {"far": 2, "middle": 1}
     q_first, last_first = {"x": 2, "middle": 1}, {"far": 2}
 
     def call(kernel, out_shape, in_specs, scratch, flops, moved, grant=40):

time: 105 us -> 105 us (level)
  no operation moved by 1% of the time
where the time goes in v6:
time: 105 us; the launch traced here: 104 us
  blocking collectives  80.5 us (77%)
  Pallas kernels  13.2 us (13%)
  starting transfers between devices  6.62 us (6%)
  waiting for transfers between devices  2.22 us (2%)
    all_to_all x5, blocking collectives, exchange(): lax.all_to_all(blocks, tuple(sizes), 0, 0, tiled=True, axis_index_groups=...  80.5 us
    pallas_call x1, Pallas kernels, body(): call(lambda *refs: factor_kernel(math.sqrt(cout), *refs), (jax.ShapeDtype...  6.75 us
    all_to_all x1, starting transfers between devices, exchange(): lax.all_to_all(blocks, tuple(sizes), 0, 0, tiled=True, axis_index_groups=...  6.62 us
    pallas_call x1, Pallas kernels, body(): call(lambda *refs: left_kernel(width, *refs), (jax.ShapeDtypeStruct((coun...  2.63 us
    pallas_call x1, Pallas kernels, body(): call(lambda *refs: right_kernel(width, *refs), jax.ShapeDtypeStruct((coun...  2.58 us
    all_to_all x1, waiting for transfers between devices, exchange(): lax.all_to_all(blocks, tuple(sizes), 0, 0, tiled=True, axis_index_groups=...  2.22 us
  transfers between devices with their start and end apart: 1, of which 1 were waited for; matrix products, arithmetic and copies ran while one was open for 1% of the time, Pallas kernels for 6%

profile of v6, /device:TPU:8, one launch (start us, length us, event | category | flops | bytes accessed | tf_op | source)
XLA Modules:
  0.0 104.4 jit_solution(15684319392811890173)
XLA Ops:
  0.6 2.6 %shard_map.50 = (f32[64,1,1280]{2,1,0:T(1,128)S(1)}, bf16[1088,160]{1,0:T(8,128)(2,1)S(1)}, bf16[1024,1280]{1,0:T(8,128)(2,1)S(1)}) custom-call(bf16[1088,160]{1,0:T(8,128)(2,1)} %bitcast.6, bf16[9,64,160]{2,1,0:T(8,128)(2,1)} %bitcast.7, bf16[1024,1280]{1,0:T(8,128)(2,1)} %bitcast.4), custom_call_target="tpu_custom_call" | custom-call | flops 671088640 | bytes 2621440 | tf_op jit(solution)/shard_map/pallas_call | solution.py:199
  3.3 18.8 %all_to_all.30 = f32[64,1,1280]{2,1,0:T(1,128)S(1)} all-to-all(f32[64,1,1280]{2,1,0:T(1,128)S(1)} %get-tuple-element.10), channel_id=1, replica_groups={{398,399,392,393,394,395,396,397,390,391,384,385,386,387,388,389,14,15,..., dimensions={0} | all-to-all | bytes 655360 | tf_op jit(solution)/shard_map/all_to_all | solution.py:182
  22.1 0.2 reduce_sum.36
  22.4 17.9 %all_to_all.31 = f32[8,1,1280]{2,1,0:T(1,128)S(1)} all-to-all(f32[8,1,1280]{2,1,0:T(1,128)S(1)} %broadcast_in_dim.8), channel_id=1, replica_groups={{80,64,112,96,16,0,48,32},{81,65,113,97,17,1,49,33},{82,66,114,98,18,2,..., dimensions={0} | all-to-all | bytes 81920 | tf_op jit(solution)/shard_map/all_to_all | solution.py:182
  40.3 0.2 broadcast_in_dim.9
  40.5 14.5 %all_to_all.32.refs_0_ = f32[64,1,1280]{2,1,0:T(1,128)S(1)} all-to-all(f32[64,1,1280]{2,1,0:T(1,128)S(1)} %broadcast_in_dim.9), channel_id=1, replica_groups={{398,399,392,393,394,395,396,397,390,391,384,385,386,387,388,389,14,15,..., dimensions={0} | all-to-all | bytes 655360 | tf_op jit(solution)/shard_map/all_to_all | solution.py:182
  54.9 2.6 %shard_map.51 = f32[16,4,1440]{2,1,0:T(4,128)} custom-call(f32[64,1,1280]{2,1,0:T(1,128)S(1)} %all_to_all.32.refs_0_, bf16[1088,160]{1,0:T(8,128)(2,1)S(1)} %get-tuple-element.11.refs_1_, bf16[1024,1280]{1,0:T(8,128)(2,1)S(1)} %get-tuple-element.12.refs_2_), custom_call_target="tpu_custom_call" | custom-call | flops 1342177280 | bytes 2621440 | tf_op jit(solution)/shard_map/pallas_call | solution.py:216
  57.5 6.6 %all-to-all-start.3 = ((f32[16,4,1440]{2,1,0:T(4,128)}), f32[16,4,1440]{2,1,0:T(4,128)S(1)}, u32[]{:S(2)}, u32[]{:S(2)}) async-start(f32[16,4,1440]{2,1,0:T(4,128)} %shard_map.51), calls=%async_computation.3 | async-start | bytes 786432 | tf_op jit(solution)/shard_map/all_to_all | solution.py:182
  64.1 6.8 %shard_map.52 = (f32[64,64]{1,0:T(8,128)S(1)}, f32[1280,64]{1,0:T(8,128)S(1)}) custom-call(f32[64,1,1280]{2,1,0:T(1,128)S(1)} %all_to_all.32.refs_0_), custom_call_target="tpu_custom_call" | custom-call | flops 671088640 | bytes 2621440 | tf_op jit(solution)/shard_map/pallas_call | solution.py:226
  70.9 0.6 constant_dynamic-slice_fusion
  71.5 2.2 %all-to-all-done.3 = f32[16,4,1440]{2,1,0:T(4,128)S(1)} async-done(((f32[16,4,1440]{2,1,0:T(4,128)}), f32[16,4,1440]{2,1,0:T(4,128)S(1)}, u32[]{:S(2)}, u32[]{:S(2)}) %all-to-all-start.3) | async-done | bytes 368672 | tf_op jit(solution)/shard_map/all_to_all | solution.py:182
  73.7 0.1 reduce_sum.38
  73.8 15.6 %all_to_all.33 = f32[4,4,1440]{2,1,0:T(4,128)S(1)} all-to-all(f32[4,4,1440]{2,1,0:T(4,128)S(1)} %broadcast_in_dim.10), channel_id=1, replica_groups={{64,96,0,32},{65,97,1,33},{66,98,2,34},{67,99,3,35},{68,100,4,36},{69,1..., dimensions={0} | all-to-all | bytes 184320 | tf_op jit(solution)/shard_map/all_to_all | solution.py:182
  89.4 0.1 broadcast_in_dim.11
  89.5 13.7 %all_to_all.34.refs_0_ = f32[16,4,1440]{2,1,0:T(4,128)S(1)} all-to-all(f32[16,4,1440]{2,1,0:T(4,128)S(1)} %broadcast_in_dim.11), channel_id=1, replica_groups={{272,280,256,264,400,408,384,392,16,24,0,8,144,152,128,136},{273,281,25..., dimensions={0} | all-to-all | bytes 737280 | tf_op jit(solution)/shard_map/all_to_all | solution.py:182
  103.2 1.2 %shard_map.53 = f32[9,64,160]{2,1,0:T(8,128)} custom-call(f32[16,4,1440]{2,1,0:T(4,128)S(1)} %all_to_all.34.refs_0_, f32[64,64]{1,0:T(8,128)S(1)} %get-tuple-element.17.refs_1_), custom_call_target="tpu_custom_call" | custom-call | flops 47185920 | bytes 737280 | tf_op jit(solution)/shard_map/pallas_call | solution.py:241
  (4 shorter events, 0.1 us)
Async XLA Ops:
  57.5 16.2 %all-to-all-start.3 = ((f32[16,4,1440]{2,1,0:T(4,128)}), f32[16,4,1440]{2,1,0:T(4,128)S(1)}, u32[]{:S(2)}, u32[]{:S(2)}) async-start(f32[16,4,1440]{2,1,0:T(4,128)} %shard_map.51), calls=%async_computation.3 | async-start | bytes 786432 | tf_op jit(solution)/shard_map/all_to_all | solution.py:182

commit v7 on v6

--- a/solution.py
+++ b/solution.py
@@ -123,17 +123,22 @@
     factor_ref[...] = (scale * rows).T
 
 
-def finish_kernel(scale, q_ref, inverse_ref, out_ref):
+def finish_kernel(scale, q_ref, inverse_ref, out_hbm, taps_ref, sems):
     groups = q_ref.shape[0]
     raw = jnp.concatenate([q_ref[i] for i in range(groups)], axis=0)
     high, middle, low = parts_of(raw)
-    inv_high, inv_middle, inv_low = parts_of(inverse_ref[...])
+    inv_high, inv_middle, inv_low = parts_of(scale * inverse_ref[...])
     left = jnp.concatenate([inv_high, inv_middle, inv_high, inv_high], axis=1)
     right = jnp.concatenate([high, high, middle, low], axis=0)
-    whole = scale * dot(left, right, ((1,), (0,)))
-    cin = out_ref.shape[2]
-    for k in range(out_ref.shape[0]):
-        out_ref[k] = whole[:, cin * k : cin * (k + 1)]
+    whole = dot(left, right, ((1,), (0,)))
+    cin = taps_ref.shape[2]
+    stores = []
+    for k in range(taps_ref.shape[0]):
+        taps_ref[k] = whole[:, cin * k : cin * (k + 1)]
+        stores.append(pltpu.make_async_copy(taps_ref.at[k], out_hbm.at[k], sems.at[k]))
+        stores[-1].start()
+    for store in stores:
+        store.wait()
 
 
 def solution(mesh):
@@ -150,12 +155,12 @@
     p_first, far_first = {"x": 3, "y": 3, "near": 1}, {"far": 2, "middle": 1}
     q_first, last_first = {"x": 2, "middle": 1}, {"far": 2}
 
-    def call(kernel, out_shape, in_specs, scratch, flops, moved, grant=40):
+    def call(kernel, out_shape, in_specs, scratch, flops, moved, grant=40, out=VMEM):
         return pl.pallas_call(
             kernel,
             out_shape=out_shape,
             in_specs=in_specs,
-            out_specs=jax.tree.map(lambda _: VMEM, out_shape),
+            out_specs=jax.tree.map(lambda _: out, out_shape),
             scratch_shapes=scratch,
             compiler_params=pltpu.CompilerParams(vmem_limit_bytes=grant * 2**20),
             cost_estimate=pl.CostEstimate(flops=flops, bytes_accessed=moved, transcendentals=0),
@@ -242,9 +247,10 @@
             lambda *refs: finish_kernel(1.0 / math.sqrt(cout), *refs),
             jax.ShapeDtypeStruct((taps, rank, cin), F32),
             [VMEM, VMEM],
-            [],
+            [pltpu.VMEM((taps, rank, cin), F32), pltpu.SemaphoreType.DMA((taps,))],
             2 * taps * cin * rank * 256,
             8 * taps * cin * rank,
+            out=HBM,
         )(q_raw, inverse)
         return p_factor, jnp.swapaxes(q_factor, 1, 2)
 

time: 105 us -> 105 us (level)
  no operation moved by 1% of the time
where the time goes in v7:
time: 105 us; the launch traced here: 104 us
  blocking collectives  80.5 us (77%)
  Pallas kernels  13.1 us (12%)
  starting transfers between devices  6.62 us (6%)
  waiting for transfers between devices  2.22 us (2%)
    all_to_all x5, blocking collectives, exchange(): lax.all_to_all(blocks, tuple(sizes), 0, 0, tiled=True, axis_index_groups=...  80.5 us
    pallas_call x1, Pallas kernels, body(): call(lambda *refs: factor_kernel(math.sqrt(cout), *refs), (jax.ShapeDtype...  6.75 us
    all_to_all x1, starting transfers between devices, exchange(): lax.all_to_all(blocks, tuple(sizes), 0, 0, tiled=True, axis_index_groups=...  6.62 us
    pallas_call x1, Pallas kernels, body(): call(lambda *refs: left_kernel(width, *refs), (jax.ShapeDtypeStruct((coun...  2.63 us
    pallas_call x1, Pallas kernels, body(): call(lambda *refs: right_kernel(width, *refs), jax.ShapeDtypeStruct((coun...  2.58 us
    all_to_all x1, waiting for transfers between devices, exchange(): lax.all_to_all(blocks, tuple(sizes), 0, 0, tiled=True, axis_index_groups=...  2.22 us
  transfers between devices with their start and end apart: 1, of which 1 were waited for; matrix products, arithmetic and copies ran while one was open for 1% of the time, Pallas kernels for 6%

profile of v7, /device:TPU:8, one launch (start us, length us, event | category | flops | bytes accessed | tf_op | source)
XLA Modules:
  0.0 104.3 jit_solution(3675009602346187080)
XLA Ops:
  0.6 2.6 %shard_map.50 = (f32[64,1,1280]{2,1,0:T(1,128)S(1)}, bf16[1088,160]{1,0:T(8,128)(2,1)S(1)}, bf16[1024,1280]{1,0:T(8,128)(2,1)S(1)}) custom-call(bf16[1088,160]{1,0:T(8,128)(2,1)} %bitcast.6, bf16[9,64,160]{2,1,0:T(8,128)(2,1)} %bitcast.7, bf16[1024,1280]{1,0:T(8,128)(2,1)} %bitcast.4), custom_call_target="tpu_custom_call" | custom-call | flops 671088640 | bytes 2621440 | tf_op jit(solution)/shard_map/pallas_call | solution.py:204
  3.3 18.8 %all_to_all.30 = f32[64,1,1280]{2,1,0:T(1,128)S(1)} all-to-all(f32[64,1,1280]{2,1,0:T(1,128)S(1)} %get-tuple-element.10), channel_id=1, replica_groups={{398,399,392,393,394,395,396,397,390,391,384,385,386,387,388,389,14,15,..., dimensions={0} | all-to-all | bytes 655360 | tf_op jit(solution)/shard_map/all_to_all | solution.py:187
  22.1 0.2 reduce_sum.36
  22.4 17.9 %all_to_all.31 = f32[8,1,1280]{2,1,0:T(1,128)S(1)} all-to-all(f32[8,1,1280]{2,1,0:T(1,128)S(1)} %broadcast_in_dim.8), channel_id=1, replica_groups={{80,64,112,96,16,0,48,32},{81,65,113,97,17,1,49,33},{82,66,114,98,18,2,..., dimensions={0} | all-to-all | bytes 81920 | tf_op jit(solution)/shard_map/all_to_all | solution.py:187
  40.3 0.2 broadcast_in_dim.9
  40.5 14.5 %all_to_all.32.refs_0_ = f32[64,1,1280]{2,1,0:T(1,128)S(1)} all-to-all(f32[64,1,1280]{2,1,0:T(1,128)S(1)} %broadcast_in_dim.9), channel_id=1, replica_groups={{398,399,392,393,394,395,396,397,390,391,384,385,386,387,388,389,14,15,..., dimensions={0} | all-to-all | bytes 655360 | tf_op jit(solution)/shard_map/all_to_all | solution.py:187
  54.9 2.6 %shard_map.51 = f32[16,4,1440]{2,1,0:T(4,128)} custom-call(f32[64,1,1280]{2,1,0:T(1,128)S(1)} %all_to_all.32.refs_0_, bf16[1088,160]{1,0:T(8,128)(2,1)S(1)} %get-tuple-element.11.refs_1_, bf16[1024,1280]{1,0:T(8,128)(2,1)S(1)} %get-tuple-element.12.refs_2_), custom_call_target="tpu_custom_call" | custom-call | flops 1342177280 | bytes 2621440 | tf_op jit(solution)/shard_map/pallas_call | solution.py:221
  57.5 6.6 %all-to-all-start.3 = ((f32[16,4,1440]{2,1,0:T(4,128)}), f32[16,4,1440]{2,1,0:T(4,128)S(1)}, u32[]{:S(2)}, u32[]{:S(2)}) async-start(f32[16,4,1440]{2,1,0:T(4,128)} %shard_map.51), calls=%async_computation.3 | async-start | bytes 786432 | tf_op jit(solution)/shard_map/all_to_all | solution.py:187
  64.1 6.8 %shard_map.52 = (f32[64,64]{1,0:T(8,128)S(1)}, f32[1280,64]{1,0:T(8,128)S(1)}) custom-call(f32[64,1,1280]{2,1,0:T(1,128)S(1)} %all_to_all.32.refs_0_), custom_call_target="tpu_custom_call" | custom-call | flops 671088640 | bytes 2621440 | tf_op jit(solution)/shard_map/pallas_call | solution.py:231
  70.9 0.6 constant_dynamic-slice_fusion
  71.5 2.2 %all-to-all-done.3 = f32[16,4,1440]{2,1,0:T(4,128)S(1)} async-done(((f32[16,4,1440]{2,1,0:T(4,128)}), f32[16,4,1440]{2,1,0:T(4,128)S(1)}, u32[]{:S(2)}, u32[]{:S(2)}) %all-to-all-start.3) | async-done | bytes 368672 | tf_op jit(solution)/shard_map/all_to_all | solution.py:187
  73.7 0.1 reduce_sum.38
  73.8 15.6 %all_to_all.33 = f32[4,4,1440]{2,1,0:T(4,128)S(1)} all-to-all(f32[4,4,1440]{2,1,0:T(4,128)S(1)} %broadcast_in_dim.10), channel_id=1, replica_groups={{64,96,0,32},{65,97,1,33},{66,98,2,34},{67,99,3,35},{68,100,4,36},{69,1..., dimensions={0} | all-to-all | bytes 184320 | tf_op jit(solution)/shard_map/all_to_all | solution.py:187
  89.4 0.1 broadcast_in_dim.11
  89.5 13.7 %all_to_all.34.refs_0_ = f32[16,4,1440]{2,1,0:T(4,128)S(1)} all-to-all(f32[16,4,1440]{2,1,0:T(4,128)S(1)} %broadcast_in_dim.11), channel_id=1, replica_groups={{272,280,256,264,400,408,384,392,16,24,0,8,144,152,128,136},{273,281,25..., dimensions={0} | all-to-all | bytes 737280 | tf_op jit(solution)/shard_map/all_to_all | solution.py:187
  103.2 1.2 %shard_map.53 = f32[9,64,160]{2,1,0:T(8,128)} custom-call(f32[16,4,1440]{2,1,0:T(4,128)S(1)} %all_to_all.34.refs_0_, f32[64,64]{1,0:T(8,128)S(1)} %get-tuple-element.17.refs_1_), custom_call_target="tpu_custom_call" | custom-call | flops 47185920 | bytes 737280 | tf_op jit(solution)/shard_map/pallas_call | solution.py:246
  (4 shorter events, 0.1 us)
Async XLA Ops:
  57.5 16.2 %all-to-all-start.3 = ((f32[16,4,1440]{2,1,0:T(4,128)}), f32[16,4,1440]{2,1,0:T(4,128)S(1)}, u32[]{:S(2)}, u32[]{:S(2)}) async-start(f32[16,4,1440]{2,1,0:T(4,128)} %shard_map.51), calls=%async_computation.3 | async-start | bytes 786432 | tf_op jit(solution)/shard_map/all_to_all | solution.py:187
